TPU v7x, 32 devices: a whole 2x2x4 slice. The times are simulated.
32 devices in a mesh: res: 8 (over y, x, core), frame: 4 (over z).
Axes of the slice: x: 2, y: 2, z: 4, core: 2. Of those that a mesh axis runs over, the one named last changes fastest.
Arguments:
- activations: bfloat16 [8, 1024, 768], P('frame', 'res'), may hold values from -6 to 6
- contacts: int32 [8, 5], replicated, may hold values from 0 to 1, as said below
- frame_index: int32 [8], replicated, may hold values from 0 to 21, as said below
- spatial_qkv: bfloat16 [768, 2304], replicated, may hold values from -8 to 8
- spatial_out: bfloat16 [768, 768], replicated, may hold values from -0.21875 to 0.21875
- time_qkv: bfloat16 [768, 2304], replicated, may hold values from -8 to 8
- time_out: bfloat16 [768, 768], replicated, may hold values from -0.21875 to 0.21875
Outputs:
- layer_out: bfloat16 [8, 1024, 768], P('frame', 'res')
Inputs may be any that keep to these rules, and one draw needn't show every extreme that they name: contacts[b, 2] = 1 for every block; contacts are symmetric, contacts[b, 2 + d] = contacts[b + d, 2 - d]; flags that name a block outside 0 to 7 are 0. Strictly increasing, frame_index[0] = 0, frame_index[7] = 21.
All inputs are finite; a program needn't handle non-finite values.
Results may differ from a plain program's by a relative error of at most 0.025.
Values may be sent and summed in bfloat16 or wider, within the bound.
A program may use at most 128 MiB of HBM per device.

v0:
```python
import jax
import jax.numpy as jnp
from jax import lax
from jax.sharding import PartitionSpec as P

HEAD = 64
HALO = 2


def shifted(block, axis, distance):
    devices = range(lax.axis_size(axis))
    route = [(i - distance, i) for i in devices if i - distance in devices]
    return lax.ppermute(block, axis, route)


def normalize(values_in):
    widened = values_in.astype(jnp.float32)
    mean_square = jnp.mean(widened * widened, axis=-1, keepdims=True)
    return (widened * lax.rsqrt(mean_square + 1e-06)).astype(jnp.bfloat16)


def rotate(entries, positions):
    half_size = HEAD // 2
    frequency = 10000.0 ** (-jnp.arange(half_size, dtype=jnp.float32) / half_size)
    angles = positions.astype(jnp.float32)[:, None] * frequency[None, :]
    cosine = jnp.cos(angles)[:, None, None, :]
    sine = jnp.sin(angles)[:, None, None, :]
    first = entries[..., :half_size]
    second = entries[..., half_size:]
    return jnp.concatenate(
        [first * cosine - second * sine, first * sine + second * cosine], axis=-1
    )


def softmax_weights(scores):
    top = jnp.max(scores, axis=-1, keepdims=True)
    expo = jnp.exp(scores - top)
    return (expo / jnp.sum(expo, axis=-1, keepdims=True)).astype(jnp.bfloat16)


def time_attend(query, keys, values):
    score_scale = HEAD ** (-0.5)
    scores = (
        jnp.einsum("frhd,grhd->rhfg", query, keys, preferred_element_type=jnp.float32) * score_scale
    )
    weights = softmax_weights(scores)
    return jnp.einsum(
        "rhfg,grhd->frhd", weights, values, preferred_element_type=jnp.float32
    ).astype(jnp.bfloat16)


def tile_scores(query, keys):
    return jnp.einsum(
        "frhd,fshd->fhrs", query, keys, preferred_element_type=jnp.float32
    ) * HEAD ** (-0.5)


def tile_values(weights, values):
    return jnp.einsum("fhrs,fshd->frhd", weights, values, preferred_element_type=jnp.float32)


def shards(activations, contacts, frame_index, spatial_qkv, spatial_out, time_qkv, time_out):
    frames_dev, block_rows, model_width = activations.shape
    head_count = model_width // HEAD
    flat = activations.reshape(frames_dev * block_rows, model_width)
    normed = normalize(flat)
    projected = jnp.dot(normed, spatial_qkv, preferred_element_type=jnp.float32).astype(
        jnp.bfloat16
    )
    projected = projected.reshape(frames_dev, block_rows, 3, head_count, HEAD)
    query = projected[:, :, 0]
    keys = projected[:, :, 1]
    values = projected[:, :, 2]
    contact_row = lax.dynamic_slice_in_dim(contacts, lax.axis_index("res"), 1, 0)[0]
    tile_list = []
    for offset in range(-HALO, HALO + 1):
        if offset == 0:
            tile_list.append((keys, values))
        else:
            tile_list.append(shifted((keys, values), "res", -offset))
    score_list = []
    for column in range(2 * HALO + 1):
        near_keys = tile_list[column][0]
        if column == HALO:
            score_list.append(tile_scores(query, near_keys))
        else:
            score_list.append(
                jnp.where(contact_row[column] > 0, tile_scores(query, near_keys), -1e30)
            )
    weights = softmax_weights(jnp.concatenate(score_list, axis=-1))
    value_shape = (frames_dev, block_rows, head_count, HEAD)
    spatial_sum = jnp.zeros(value_shape, jnp.float32)
    for column in range(2 * HALO + 1):
        part_weights = weights[..., column * block_rows : (column + 1) * block_rows]
        near_values = tile_list[column][1]
        spatial_sum = spatial_sum + tile_values(part_weights, near_values)
    spatial_mix = spatial_sum.astype(jnp.bfloat16).reshape(frames_dev * block_rows, model_width)
    hidden = (
        flat.astype(jnp.float32)
        + jnp.dot(spatial_mix, spatial_out, preferred_element_type=jnp.float32)
    ).astype(jnp.bfloat16)
    renormed = normalize(hidden)
    time_projected = jnp.dot(renormed, time_qkv, preferred_element_type=jnp.float32).astype(
        jnp.bfloat16
    )
    time_projected = time_projected.reshape(frames_dev, block_rows, 3, head_count, HEAD)
    first_frame = lax.axis_index("frame") * frames_dev
    positions = lax.dynamic_slice_in_dim(frame_index, first_frame, frames_dev, 0)
    time_query = rotate(time_projected[:, :, 0].astype(jnp.float32), positions).astype(jnp.bfloat16)
    time_keys = rotate(time_projected[:, :, 1].astype(jnp.float32), positions).astype(jnp.bfloat16)
    time_values = time_projected[:, :, 2]
    all_keys, all_values = (
        lax.all_gather(time_keys, "frame", axis=0, tiled=True),
        lax.all_gather(time_values, "frame", axis=0, tiled=True),
    )
    time_mix = time_attend(time_query, all_keys, all_values)
    time_mix = time_mix.reshape(frames_dev * block_rows, model_width)
    layer_out = hidden.astype(jnp.float32) + jnp.dot(
        time_mix, time_out, preferred_element_type=jnp.float32
    )
    return layer_out.astype(jnp.bfloat16).reshape(frames_dev, block_rows, model_width)


def solution(mesh):
    placed = (P("frame", "res", None), P(), P(), P(), P(), P(), P())
    return jax.shard_map(
        shards, mesh=mesh, in_specs=placed, out_specs=P("frame", "res", None), check_vma=False
    )
```

profile of v0, /device:TPU:3, one launch (start us, length us, event | category | flops | bytes accessed | tf_op | source)
XLA Modules:
  0.0 209.3 jit_solution(17792526123560342739)
XLA Ops:
  9.0 2.1 %convolution_convert_fusion.1 = bf16[256,2304]{1,0:T(8,128)(2,1)} fusion(bf16[256,768]{1,0:T(8,128)(2,1)S(1)} %fusion.30, bf16[768,2304]{1,0:T(8,128)(2,1)S(1)} %copy-done), kind=kOutput, calls=%fused_computation.5 | convolution fusion | flops 906559488 | bytes 5111808 | tf_op jit(solution)/shard_map/dot_general | solution.py:67
  11.1 2.4 %copy.34 = bf16[256,2304]{0,1:T(8,128)(2,1)} copy(bf16[256,2304]{1,0:T(8,128)(2,1)} %convolution_convert_fusion.1) | data formatting | bytes 2359296 | tf_op jit(solution)/shard_map/convert_element_type | solution.py:67
  13.5 3.5 %reshape.131 = bf16[2,128,3,12,64]{1,0,4,3,2:T(2,128)(2,1)} reshape(bf16[256,2304]{0,1:T(8,128)(2,1)} %copy.34) | data formatting | bytes 2359296 | tf_op jit(solution)/shard_map/reshape | solution.py:70
  17.1 2.9 %fusion.44 = (bf16[2,128,1,12,64]{1,0,4,3,2:T(2,128)(2,1)}, bf16[2,128,1,12,64]{1,0,4,3,2:T(2,128)(2,1)S(1)}, bf16[2,128,1,12,64]{1,0,4,3,2:T(2,128)(2,1)S(1)}) fusion(bf16[2,128,3,12,64]{1,0,4,3,2:T(2,128)(2,1)} %reshape.131), kind=kLoop, calls=%fused_computation.82 | loop fusion | bytes 2359296 | tf_op jit(solution)/shard_map/slice | solution.py:71
  21.6 3.1 %collective-permute-start.1 = (bf16[2,128,12,64]{1,3,2,0:T(8,128)(2,1)}, bf16[2,128,12,64]{1,3,2,0:T(8,128)(2,1)}, u32[]{:S(2)}, u32[]{:S(2)}) collective-permute-start(bf16[2,128,12,64]{1,3,2,0:T(8,128)(2,1)} %bitcast.88), channel_id=1, source_target_pairs={{0,8},{4,12},{8,16},{12,20},{16,24},{20,28},{1,9},{5,13},{9,17},{1... | collective-permute-start | bytes 1179656 | tf_op jit(solution)/shard_map/ppermute | solution.py:13
  24.7 4.0 %collective-permute-start.2 = (bf16[2,128,12,64]{1,3,2,0:T(8,128)(2,1)}, bf16[2,128,12,64]{1,3,2,0:T(8,128)(2,1)}, u32[]{:S(2)}, u32[]{:S(2)}) collective-permute-start(bf16[2,128,12,64]{1,3,2,0:T(8,128)(2,1)} %bitcast.88), channel_id=1, source_target_pairs={{0,4},{4,8},{8,12},{12,16},{16,20},{20,24},{24,28},{1,5},{5,9},{9,... | collective-permute-start | bytes 1179656 | tf_op jit(solution)/shard_map/ppermute | solution.py:13
  28.7 1.9 collective-permute-start.3
  30.6 2.2 %collective-permute-start.4 = (bf16[2,128,12,64]{1,3,2,0:T(8,128)(2,1)}, bf16[2,128,12,64]{1,3,2,0:T(8,128)(2,1)}, u32[]{:S(2)}, u32[]{:S(2)}) collective-permute-start(bf16[2,128,12,64]{1,3,2,0:T(8,128)(2,1)} %bitcast.88), channel_id=1, source_target_pairs={{8,0},{12,4},{16,8},{20,12},{24,16},{28,20},{9,1},{13,5},{17,9},{2... | collective-permute-start | bytes 1179656 | tf_op jit(solution)/shard_map/ppermute | solution.py:13
  33.6 4.8 %collective-permute-start.5 = (bf16[2,128,12,64]{1,3,2,0:T(8,128)(2,1)}, bf16[2,128,12,64]{1,3,2,0:T(8,128)(2,1)}, u32[]{:S(2)}, u32[]{:S(2)}) collective-permute-start(bf16[2,128,12,64]{1,3,2,0:T(8,128)(2,1)} %bitcast.89), channel_id=1, source_target_pairs={{0,4},{4,8},{8,12},{12,16},{16,20},{20,24},{24,28},{1,5},{5,9},{9,... | collective-permute-start | bytes 1179656 | tf_op jit(solution)/shard_map/ppermute | solution.py:13
  42.7 3.9 %collective-permute-start = (bf16[2,128,12,64]{1,3,2,0:T(8,128)(2,1)}, bf16[2,128,12,64]{1,3,2,0:T(8,128)(2,1)S(1)}, u32[]{:S(2)}, u32[]{:S(2)}) collective-permute-start(bf16[2,128,12,64]{1,3,2,0:T(8,128)(2,1)} %bitcast.89), channel_id=1, source_target_pairs={{0,8},{4,12},{8,16},{12,20},{16,24},{20,28},{1,9},{5,13},{9,17},{1... | collective-permute-start | bytes 1179656 | tf_op jit(solution)/shard_map/ppermute | solution.py:13
  48.2 2.1 collective-permute-start.7
  52.1 2.1 %collective-permute-start.6 = (bf16[2,128,12,64]{1,3,2,0:T(8,128)(2,1)}, bf16[2,128,12,64]{1,3,2,0:T(8,128)(2,1)S(1)}, u32[]{:S(2)}, u32[]{:S(2)}) collective-permute-start(bf16[2,128,12,64]{1,3,2,0:T(8,128)(2,1)} %bitcast.89), channel_id=1, source_target_pairs={{4,0},{8,4},{12,8},{16,12},{20,16},{24,20},{28,24},{5,1},{9,5},{13... | collective-permute-start | bytes 1179656 | tf_op jit(solution)/shard_map/ppermute | solution.py:13
  61.4 15.1 %collective-permute-done.7 = bf16[2,128,12,64]{1,3,2,0:T(8,128)(2,1)S(1)} collective-permute-done((bf16[2,128,12,64]{1,3,2,0:T(8,128)(2,1)}, bf16[2,128,12,64]{1,3,2,0:T(8,128)(2,1)S(1)}, u32[]{:S(2)}, u32[]{:S(2)}) %collective-permute-start.7) | collective-permute-done | bytes 393248 | tf_op jit(solution)/shard_map/ppermute | solution.py:13
  80.1 2.2 %convolution_convert_fusion = bf16[256,2304]{1,0:T(8,128)(2,1)} fusion(bf16[768,2304]{1,0:T(8,128)(2,1)S(1)} %copy-done.8, f32[256,768]{1,0:T(8,128)S(1)} %get-tuple-element.34, f32[256]{0:T(256)S(1)} %add_rsqrt_fusion), kind=kOutput, calls=%fused_computation.4 | convolution fusion | flops 906952704 | bytes 5506048 | tf_op jit(solution)/shard_map/dot_general | solution.py:103
  82.2 2.4 %copy.44 = bf16[256,2304]{0,1:T(8,128)(2,1)} copy(bf16[256,2304]{1,0:T(8,128)(2,1)} %convolution_convert_fusion) | data formatting | bytes 2359296 | tf_op jit(solution)/shard_map/convert_element_type | solution.py:103
  84.6 3.5 %reshape.133 = bf16[2,128,3,12,64]{1,0,4,3,2:T(2,128)(2,1)} reshape(bf16[256,2304]{0,1:T(8,128)(2,1)} %copy.44) | data formatting | bytes 2359296 | tf_op jit(solution)/shard_map/reshape | solution.py:106
  88.2 3.2 %fusion.43 = (bf16[2,128,1,12,64]{1,0,4,3,2:T(2,128)(2,1)}, bf16[2,128,1,12,64]{1,0,4,3,2:T(2,128)(2,1)}, bf16[2,128,1,12,64]{1,0,4,3,2:T(2,128)(2,1)}) fusion(bf16[2,128,3,12,64]{1,0,4,3,2:T(2,128)(2,1)} %reshape.133), kind=kLoop, calls=%fused_computation.81 | loop fusion | bytes 2359296 | tf_op jit(solution)/shard_map/slice | solution.py:109
  91.4 3.1 %copy.60 = bf16[2,128,1,12,64]{4,0,3,1,2:T(2,128)(2,1)} copy(bf16[2,128,1,12,64]{1,0,4,3,2:T(2,128)(2,1)} %get-tuple-element.19) | data formatting | bytes 786432
  94.5 3.1 %copy.61 = bf16[2,128,1,12,64]{4,0,3,1,2:T(2,128)(2,1)} copy(bf16[2,128,1,12,64]{1,0,4,3,2:T(2,128)(2,1)} %get-tuple-element.20) | data formatting | bytes 786432
  97.7 2.4 %bitcast_convert_fusion = (f32[2,128,12,64]{3,0,2,1:T(2,128)S(1)}, f32[2,128,12,64]{3,0,2,1:T(2,128)S(1)}) fusion(bf16[2,128,1,12,64]{4,0,3,1,2:T(2,128)(2,1)} %copy.61, bf16[2,128,1,12,64]{4,0,3,1,2:T(2,128)(2,1)} %copy.60), kind=kLoop, calls=%fused_computation.46 | loop fusion | flops 393216 | bytes 2359296 | tf_op jit(solution)/shard_map/convert_element_type | solution.py:110
  100.1 5.0 %subtract_convert_fusion.1 = (bf16[2,128,12,32]{3,0,2,1:T(2,128)(2,1)}, bf16[2,128,12,32]{3,0,2,1:T(2,128)(2,1)}, bf16[2,128,12,32]{3,0,2,1:T(2,128)(2,1)S(1)}, bf16[2,128,12,32]{3,0,2,1:T(2,128)(2,1)S(1)}) fusion(f32[2,128,12,64]{3,0,2,1:T(2,128)S(1)} %get-tuple-element.38, f32[2,32]{1,0:T(2,128)S(1)} %get-tuple-element.28, ...), kind=kLoop, calls=%fused_computation.12 | loop fusion | flops 1572864 | bytes 2359808 | tf_op jit(solution)/shard_map/convert.5
  105.1 3.0 %pad_maximum_fusion = bf16[2,128,12,64]{3,0,2,1:T(2,128)(2,1)} fusion(bf16[2,128,12,32]{3,0,2,1:T(2,128)(2,1)S(1)} %get-tuple-element.25, bf16[2,128,12,32]{3,0,2,1:T(2,128)(2,1)S(1)} %get-tuple-element.26), kind=kLoop, calls=%fused_computation.45 | loop fusion | flops 786432 | bytes 786432 | tf_op jit(solution)/shard_map/concatenate | solution.py:30
  108.1 3.0 %copy.49 = bf16[2,128,12,64]{1,3,2,0:T(8,128)(2,1)} copy(bf16[2,128,12,64]{3,0,2,1:T(2,128)(2,1)} %pad_maximum_fusion) | data formatting | bytes 786432 | tf_op jit(solution)/shard_map/concatenate | solution.py:30
  111.1 1.8 copy.45
  113.0 35.0 %all-gather.4.cloned.1.call-done = bf16[8,128,12,64]{1,3,2,0:T(8,128)(2,1)} async-done(((bf16[2,128,12,64]{1,3,2,0:T(8,128)(2,1)}), bf16[8,128,12,64]{1,3,2,0:T(8,128)(2,1)}) %all-gather.4.cloned.1.call-update) | async-done | bytes 1572880 | tf_op jit(solution)/shard_map/all_gather | solution.py:113
  148.0 6.2 %copy.50 = bf16[8,128,12,64]{3,0,2,1:T(8,128)(2,1)} copy(bf16[8,128,12,64]{1,3,2,0:T(8,128)(2,1)} %all-gather.4.cloned.1.call-done) | data formatting | bytes 3145728 | tf_op jit(solution)/shard_map/all_gather | solution.py:113
  154.1 9.1 %fusion.46 = (f32[128,12,2]{2,1,0:T(8,128)}, f32[128,12,2,8]{3,2,1,0:T(2,128)}) fusion(bf16[8,128,12,64]{3,0,2,1:T(8,128)(2,1)} %copy.50, bf16[2,128,12,32]{3,0,2,1:T(2,128)(2,1)} %get-tuple-element.6, bf16[2,128,12,32]{3,0,2,1:T(2,128)(2,1)} %get-tuple-element.5), kind=kOutput, calls=%fused_computation.84 | convolution fusion | flops 4005895 | bytes 2076672 | tf_op jit(solution)/shard_map/sub | solution.py:37
  163.2 22.3 %all-gather.6.cloned.1.call-done = bf16[8,128,1,12,64]{1,4,3,2,0:T(8,128)(2,1)} async-done(((bf16[2,128,1,12,64]{1,4,3,2,0:T(8,128)(2,1)}), bf16[8,128,1,12,64]{1,4,3,2,0:T(8,128)(2,1)}) %all-gather.6.cloned.1.call-update) | async-done | bytes 1572880 | tf_op jit(solution)/shard_map/all_gather | solution.py:114
  185.5 6.2 %copy.46 = bf16[8,128,1,12,64]{4,0,3,1,2:T(8,128)(2,1)} copy(bf16[8,128,1,12,64]{1,4,3,2,0:T(8,128)(2,1)} %all-gather.6.cloned.1.call-done) | data formatting | bytes 3145728 | tf_op jit(solution)/shard_map/all_gather | solution.py:114
  191.7 4.9 %fusion.9 = bf16[2,128,12,64]{3,0,2,1:T(2,128)(2,1)} fusion(bf16[8,128,1,12,64]{4,0,3,1,2:T(8,128)(2,1)} %copy.46, f32[128,12,2,8]{3,2,1,0:T(2,128)} %get-tuple-element.36, f32[128,12,2]{2,1,0:T(8,128)} %get-tuple-element.35), kind=kOutput, calls=%fused_computation.22 | convolution fusion | flops 3391488 | bytes 2076672 | tf_op jit(solution)/shard_map/rhfg,grhd->frhd/dot_general | solution.py:47
  196.6 3.1 %copy.51 = bf16[2,128,12,64]{1,0,3,2:T(2,128)(2,1)} copy(bf16[2,128,12,64]{3,0,2,1:T(2,128)(2,1)} %fusion.9) | data formatting | bytes 786432 | tf_op jit(solution)/shard_map/convert_element_type | solution.py:49
  199.6 2.9 %fusion.16 = bf16[256,768]{1,0:T(8,128)(2,1)} fusion(f32[256,768]{1,0:T(8,128)} %copy-done.7, bf16[768,768]{1,0:T(8,128)(2,1)} %param.13, bf16[96,8,2,128]{3,2,1,0:T(2,128)(2,1)} %bitcast.91), kind=kOutput, calls=%fused_computation.31 | convolution fusion | flops 302383104 | bytes 2752512 | tf_op jit(solution)/shard_map/dot_general | solution.py:118
  (59 shorter events, 20.6 us)
Async XLA Ops:
  6.5 2.5 %copy-start = (bf16[768,2304]{1,0:T(8,128)(2,1)S(1)}, bf16[768,2304]{1,0:T(8,128)(2,1)}, u32[]{:S(2)}) copy-start(bf16[768,2304]{1,0:T(8,128)(2,1)} %param.10) | copy-start | bytes 10616836
  6.5 141.4 %all-gather.4.cloned.1.call-start = ((), (), s32[]{:S(2)}) async-start(), calls=%async_computation | async-start | bytes 1966080 | tf_op jit(solution)/shard_map/all_gather | solution.py:113
  17.1 22.1 %copy-start.10 = (s32[8]{0:T(128)S(1)}, s32[8]{0:T(128)}, u32[]{:S(2)}) copy-start(s32[8]{0:T(128)} %param.9) | copy-start | bytes 100
  20.0 0.8 copy-start.1
  20.0 12.8 %copy-start.3 = (bf16[2,128,1,12,64]{1,0,4,3,2:T(2,128)(2,1)}, bf16[2,128,1,12,64]{1,0,4,3,2:T(2,128)(2,1)S(1)}, u32[]{:S(2)}) copy-start(bf16[2,128,1,12,64]{1,0,4,3,2:T(2,128)(2,1)S(1)} %get-tuple-element.23) | copy-start | bytes 1179652
  21.6 21.1 %collective-permute-start.1 = (bf16[2,128,12,64]{1,3,2,0:T(8,128)(2,1)}, bf16[2,128,12,64]{1,3,2,0:T(8,128)(2,1)}, u32[]{:S(2)}, u32[]{:S(2)}) collective-permute-start(bf16[2,128,12,64]{1,3,2,0:T(8,128)(2,1)} %bitcast.88), channel_id=1, source_target_pairs={{0,8},{4,12},{8,16},{12,20},{16,24},{20,28},{1,9},{5,13},{9,17},{1... | collective-permute-start | bytes 1179656 | tf_op jit(solution)/shard_map/ppermute | solution.py:13
  24.7 23.5 %collective-permute-start.2 = (bf16[2,128,12,64]{1,3,2,0:T(8,128)(2,1)}, bf16[2,128,12,64]{1,3,2,0:T(8,128)(2,1)}, u32[]{:S(2)}, u32[]{:S(2)}) collective-permute-start(bf16[2,128,12,64]{1,3,2,0:T(8,128)(2,1)} %bitcast.88), channel_id=1, source_target_pairs={{0,4},{4,8},{8,12},{12,16},{16,20},{20,24},{24,28},{1,5},{5,9},{9,... | collective-permute-start | bytes 1179656 | tf_op jit(solution)/shard_map/ppermute | solution.py:13
  28.7 23.5 %collective-permute-start.3 = (bf16[2,128,12,64]{1,3,2,0:T(8,128)(2,1)}, bf16[2,128,12,64]{1,3,2,0:T(8,128)(2,1)}, u32[]{:S(2)}, u32[]{:S(2)}) collective-permute-start(bf16[2,128,12,64]{1,3,2,0:T(8,128)(2,1)} %bitcast.88), channel_id=1, source_target_pairs={{4,0},{8,4},{12,8},{16,12},{20,16},{24,20},{28,24},{5,1},{9,5},{13... | collective-permute-start | bytes 1179656 | tf_op jit(solution)/shard_map/ppermute | solution.py:13
  30.6 25.1 %collective-permute-start.4 = (bf16[2,128,12,64]{1,3,2,0:T(8,128)(2,1)}, bf16[2,128,12,64]{1,3,2,0:T(8,128)(2,1)}, u32[]{:S(2)}, u32[]{:S(2)}) collective-permute-start(bf16[2,128,12,64]{1,3,2,0:T(8,128)(2,1)} %bitcast.88), channel_id=1, source_target_pairs={{8,0},{12,4},{16,8},{20,12},{24,16},{28,20},{9,1},{13,5},{17,9},{2... | collective-permute-start | bytes 1179656 | tf_op jit(solution)/shard_map/ppermute | solution.py:13
  33.6 26.4 %collective-permute-start.5 = (bf16[2,128,12,64]{1,3,2,0:T(8,128)(2,1)}, bf16[2,128,12,64]{1,3,2,0:T(8,128)(2,1)}, u32[]{:S(2)}, u32[]{:S(2)}) collective-permute-start(bf16[2,128,12,64]{1,3,2,0:T(8,128)(2,1)} %bitcast.89), channel_id=1, source_target_pairs={{0,4},{4,8},{8,12},{12,16},{16,20},{20,24},{24,28},{1,5},{5,9},{9,... | collective-permute-start | bytes 1179656 | tf_op jit(solution)/shard_map/ppermute | solution.py:13
  39.2 11.1 %copy-start.5 = (bf16[2,128,1,12,64]{1,0,4,3,2:T(2,128)(2,1)S(1)}, bf16[2,128,1,12,64]{1,0,4,3,2:T(2,128)(2,1)}, u32[]{:S(2)}) copy-start(bf16[2,128,1,12,64]{1,0,4,3,2:T(2,128)(2,1)} %get-tuple-element.22) | copy-start | bytes 1179652
  42.7 34.1 %collective-permute-start = (bf16[2,128,12,64]{1,3,2,0:T(8,128)(2,1)}, bf16[2,128,12,64]{1,3,2,0:T(8,128)(2,1)S(1)}, u32[]{:S(2)}, u32[]{:S(2)}) collective-permute-start(bf16[2,128,12,64]{1,3,2,0:T(8,128)(2,1)} %bitcast.89), channel_id=1, source_target_pairs={{0,8},{4,12},{8,16},{12,20},{16,24},{20,28},{1,9},{5,13},{9,17},{1... | collective-permute-start | bytes 1179656 | tf_op jit(solution)/shard_map/ppermute | solution.py:13
  48.1 3.6 %copy-start.2 = (bf16[2,128,1,12,64]{1,0,4,3,2:T(2,128)(2,1)S(1)}, bf16[2,128,1,12,64]{1,0,4,3,2:T(2,128)(2,1)}, u32[]{:S(2)}) copy-start(bf16[2,128,1,12,64]{1,0,4,3,2:T(2,128)(2,1)} %copy-done.1) | copy-start | bytes 1179652
  48.2 28.3 %collective-permute-start.7 = (bf16[2,128,12,64]{1,3,2,0:T(8,128)(2,1)}, bf16[2,128,12,64]{1,3,2,0:T(8,128)(2,1)S(1)}, u32[]{:S(2)}, u32[]{:S(2)}) collective-permute-start(bf16[2,128,12,64]{1,3,2,0:T(8,128)(2,1)} %bitcast.89), channel_id=1, source_target_pairs={{8,0},{12,4},{16,8},{20,12},{24,16},{28,20},{9,1},{13,5},{17,9},{2... | collective-permute-start | bytes 1179656 | tf_op jit(solution)/shard_map/ppermute | solution.py:13
  52.1 25.5 %collective-permute-start.6 = (bf16[2,128,12,64]{1,3,2,0:T(8,128)(2,1)}, bf16[2,128,12,64]{1,3,2,0:T(8,128)(2,1)S(1)}, u32[]{:S(2)}, u32[]{:S(2)}) collective-permute-start(bf16[2,128,12,64]{1,3,2,0:T(8,128)(2,1)} %bitcast.89), channel_id=1, source_target_pairs={{4,0},{8,4},{12,8},{16,12},{20,16},{24,20},{28,24},{5,1},{9,5},{13... | collective-permute-start | bytes 1179656 | tf_op jit(solution)/shard_map/ppermute | solution.py:13
  58.3 1.4 copy-start.4
  77.1 1.2 copy-start.6
  77.1 1.4 copy-start.9
  78.0 2.1 %copy-start.8 = (bf16[768,2304]{1,0:T(8,128)(2,1)S(1)}, bf16[768,2304]{1,0:T(8,128)(2,1)}, u32[]{:S(2)}) copy-start(bf16[768,2304]{1,0:T(8,128)(2,1)} %param.12) | copy-start | bytes 10616836
  79.1 0.9 copy-start.7
  111.1 74.4 %all-gather.6.cloned.1.call-start = ((), (), s32[]{:S(2)}) async-start(), calls=%async_computation.1 | async-start | bytes 1966080 | tf_op jit(solution)/shard_map/all_gather | solution.py:114
Sparse Core Ops, SparseCore 0:
  111.2 36.7 all-gather.3
  149.5 35.9 all-gather.5
where the time goes:
time: 212 us; the launch traced here: 209 us
  waiting for transfers between devices  72.9 us (34%)
  local copies, waits for them, and re-layouts  49.7 us (23%)
  matrix products  30.8 us (15%)
  starting transfers between devices  24 us (11%)
  between operations  16.4 us (8%)
  other arithmetic  15.5 us (7%)
    all_gather x1, waiting for transfers between devices, shards(): lax.all_gather(time_keys, 'frame', axis=0, tiled=True)  35 us
    ppermute x8, starting transfers between devices, shifted(): return lax.ppermute(block, axis, route)  24 us
    all_gather x1, waiting for transfers between devices, shards(): lax.all_gather(time_values, 'frame', axis=0, tiled=True)  22.3 us
    ppermute x8, waiting for transfers between devices, shifted(): return lax.ppermute(block, axis, route)  15.6 us
    unnamed x26, local copies, waits for them, and re-layouts  9.82 us
    sub x1, matrix products, softmax_weights(): expo = jnp.exp(scores - top)  9.1 us
    dot_general x5, matrix products, tile_scores(): jnp.einsum('frhd,fshd->fhrs', query, keys, preferred_element_type=jnp.flo...  6.36 us
    all_gather x1, local copies, waits for them, and re-layouts, shards(): lax.all_gather(time_keys, 'frame', axis=0, tiled=True)  6.16 us
  transfers between devices with their start and end apart: 10, of which 4 were waited for; matrix products, arithmetic and copies ran while one was open for 15% of the time, Pallas kernels for 0%

commit v1 on v0

v1 whole, which is shorter than its diff:
```python
import functools
import math

import jax
import jax.numpy as jnp
from jax import lax
from jax.experimental import pallas as pl
from jax.experimental.pallas import tpu as pltpu
from jax.sharding import PartitionSpec as P

HEAD = 64
HALO = 2
PAIR = 2 * HEAD
OWN, NEAR, BELOW, ABOVE, FAR = range(5)
F32 = jnp.float32
BF16 = jnp.bfloat16


def normalize(values_in):
    widened = values_in.astype(F32)
    mean_square = jnp.mean(widened * widened, axis=-1, keepdims=True)
    return (widened * lax.rsqrt(mean_square + 1e-06)).astype(BF16)


def attend(query, keys, values, bias):
    rows = query.shape[0]
    lanes = lax.broadcasted_iota(jnp.int32, (1, PAIR), 1)
    first = jnp.where(lanes < HEAD, HEAD ** (-0.5), 0.0).astype(BF16)
    second = jnp.where(lanes < HEAD, 0.0, HEAD ** (-0.5)).astype(BF16)
    both = jnp.concatenate([query * first, query * second], axis=0)
    scores = (
        lax.dot_general(both, keys, (((1,), (1,)), ((), ())), preferred_element_type=F32) + bias
    )
    top = jnp.max(scores, axis=-1, keepdims=True)
    expo = jnp.exp(scores - top).astype(BF16)
    wide = jnp.concatenate([values, jnp.ones_like(values)], axis=1)
    mixed = jnp.dot(expo, wide, preferred_element_type=F32)
    low = lax.broadcasted_iota(jnp.int32, (rows, PAIR), 1) < HEAD
    total = jnp.where(low, mixed[:rows, :PAIR], mixed[rows:, :PAIR])
    count = jnp.where(low, mixed[:rows, PAIR:], mixed[rows:, PAIR:])
    return (total / count).astype(BF16)


def kernel(
    res_size, frame_size,
    acts, contacts, frame_index, sqkv_in, sout_in, tqkv_in, tout_in, out_ref,
    sqkv, sout, tqkv, tout, near, query, keys, values, mix, hidden, gathered, staged, landed,
    tquery, tkeys, tvalues, cosine, sine, same,
    weight_sem, halo_send, halo_recv, frame_send, frame_recv, back_send, back_recv,
):
    frames_dev, block, width = acts.shape
    heads = width // PAIR
    share = block // frame_size
    frames = frames_dev * frame_size
    chunk = frames_dev * share
    me = lax.axis_index("res")
    slot = lax.axis_index("frame")
    odd = lax.rem(me, 2)
    mate = me + 1 - 2 * odd
    has_below = me >= HALO
    has_above = me < res_size - HALO
    has_far = jnp.where(odd == 1, me + 1 < res_size, me >= 1)
    gives_far = jnp.where(odd == 1, has_below, has_above)

    weights = [
        pltpu.make_async_copy(source, target, weight_sem.at[i])
        for i, (source, target) in enumerate(
            [(sqkv_in, sqkv), (sout_in, sout), (tqkv_in, tqkv), (tout_in, tout)]
        )
    ]
    for copy in weights:
        copy.start()

    barrier = pltpu.get_barrier_semaphore()

    def greet(res, frame):
        pl.semaphore_signal(
            barrier, inc=1, device_id=(res, frame), device_id_type=pl.DeviceIdType.MESH
        )

    greet(mate, slot)

    @pl.when(has_below)
    def _():
        greet(me - HALO, slot)

    @pl.when(has_above)
    def _():
        greet(me + HALO, slot)

    for step in range(1, frame_size):
        greet(me, lax.rem(slot + step, frame_size))

    for f in range(frames_dev):
        near[f, OWN] = normalize(acts[f])

    pl.semaphore_wait(
        barrier, frame_size + has_below.astype(jnp.int32) + has_above.astype(jnp.int32)
    )

    def halo(f, source, target, place):
        return pltpu.make_async_remote_copy(
            src_ref=near.at[f, source],
            dst_ref=near.at[f, place],
            send_sem=halo_send.at[f, place],
            recv_sem=halo_recv.at[f, place],
            device_id=(target, slot),
            device_id_type=pl.DeviceIdType.MESH,
        )

    def to_mate(f):
        return halo(f, OWN, mate, NEAR)

    def to_above(f):
        return halo(f, OWN, me + HALO, BELOW)

    def to_below(f):
        return halo(f, OWN, me - HALO, ABOVE)

    def hand_on(f):
        return halo(f, ABOVE - odd, mate, FAR)

    for f in range(frames_dev):

        @pl.when(has_above)
        def _():
            to_above(f).start()

        @pl.when(has_below)
        def _():
            to_below(f).start()

        to_mate(f).start()

    for place, there in ((BELOW, has_below), (ABOVE, has_above), (FAR, has_far)):

        @pl.when(jnp.logical_not(there))
        def _():
            near[:, place] = jnp.zeros((frames_dev, block, width), BF16)

    size = frames * share
    lane = lax.broadcasted_iota(jnp.int32, (frames, PAIR), 1)
    row = lax.broadcasted_iota(jnp.int32, (frames, PAIR), 0)
    frequency = jnp.exp(lax.rem(lane, HEAD // 2).astype(F32) * (-math.log(10000.0) / (HEAD // 2)))
    position = jnp.zeros((frames, PAIR), F32)
    for g in range(frames):
        position = jnp.where(row == g, frame_index[g].astype(F32), position)
    angle = position * frequency
    for table, entries in ((cosine, jnp.cos(angle)), (sine, jnp.sin(angle))):
        table[...] = jnp.broadcast_to(entries[:, None, :], (frames, share, PAIR)).reshape(
            size, PAIR
        )
    row = lax.broadcasted_iota(jnp.int32, (2 * chunk, size), 0)
    column = lax.broadcasted_iota(jnp.int32, (2 * chunk, size), 1)
    same[...] = jnp.where(lax.rem(row, share) == lax.rem(column, share), 0.0, -1e30)
    row = lax.broadcasted_iota(jnp.int32, (PAIR, PAIR), 0)
    column = lax.broadcasted_iota(jnp.int32, (PAIR, PAIR), 1)
    upper = lax.rem(column, HEAD) >= HEAD // 2
    turn = jnp.where(
        upper,
        jnp.where(row == column - HEAD // 2, 1.0, 0.0),
        jnp.where(row == column + HEAD // 2, -1.0, 0.0),
    ).astype(BF16)
    order = (HALO, 3 - 2 * odd, 0, 2 * HALO, 1 + 2 * odd)
    bias = jnp.concatenate(
        [
            jnp.full((1, block), jnp.where(contacts[me, place] > 0, 0.0, -1e30), F32)
            for place in order
        ],
        axis=1,
    )

    def project(f, first, count):
        rows = near[f, first : first + count].reshape(count * block, width)
        span = slice(first * block, (first + count) * block)
        for part, target in ((1, keys), (2, values)):
            target[f, span] = jnp.dot(
                rows, sqkv[:, part * width : (part + 1) * width], preferred_element_type=F32
            ).astype(BF16)

    weights[0].wait()
    for f in range(frames_dev):
        query[f] = jnp.dot(near[f, OWN], sqkv[:, :width], preferred_element_type=F32).astype(BF16)
        to_mate(f).wait_recv()
        project(f, OWN, 2)

    def frame_copy(f, step):
        peer = lax.rem(slot + step, frame_size)
        return pltpu.make_async_remote_copy(
            src_ref=hidden.at[f, pl.ds(pl.multiple_of(peer * share, 16), share)],
            dst_ref=gathered.at[slot * frames_dev + f],
            send_sem=frame_send.at[f, peer],
            recv_sem=frame_recv.at[f, slot],
            device_id=(me, peer),
            device_id_type=pl.DeviceIdType.MESH,
        )

    def frame_arrival(f, step):
        peer = lax.rem(slot + step, frame_size)
        return pltpu.make_async_remote_copy(
            src_ref=hidden.at[f, pl.ds(0, share)],
            dst_ref=gathered.at[peer * frames_dev + f],
            send_sem=frame_send.at[f, peer],
            recv_sem=frame_recv.at[f, peer],
            device_id=(me, peer),
            device_id_type=pl.DeviceIdType.MESH,
        )

    mine = pl.ds(pl.multiple_of(slot * share, 16), share)
    for f in range(frames_dev):

        @pl.when(has_below)
        def _():
            to_above(f).wait_recv()

        @pl.when(has_above)
        def _():
            to_below(f).wait_recv()

        @pl.when(gives_far)
        def _():
            hand_on(f).start()

        project(f, BELOW, 2)

        @pl.when(has_far)
        def _():
            hand_on(f).wait_recv()

        project(f, FAR, 1)
        for pair in range(heads):
            span = slice(pair * PAIR, (pair + 1) * PAIR)
            mix[:, span] = attend(query[f, :, span], keys[f, :, span], values[f, :, span], bias)
        if f == 0:
            weights[1].wait()
        hidden[f] = (
            acts[f].astype(F32) + jnp.dot(mix[...], sout[...], preferred_element_type=F32)
        ).astype(BF16)
        for step in range(1, frame_size):
            frame_copy(f, step).start()
        gathered[slot * frames_dev + f] = hidden[f, mine]

    weights[2].wait()
    weights[3].wait()
    for f in range(frames_dev):
        for step in range(1, frame_size):
            frame_arrival(f, step).wait_recv()
    renormed = normalize(gathered[...].reshape(size, width))
    for part, target in ((0, tquery), (1, tkeys), (2, tvalues)):
        projected = jnp.dot(
            renormed, tqkv[:, part * width : (part + 1) * width], preferred_element_type=F32
        ).astype(BF16)
        if part == 2:
            target[...] = projected
        else:
            for pair in range(heads):
                span = slice(pair * PAIR, (pair + 1) * PAIR)
                piece = projected[:, span]
                turned = jnp.dot(piece, turn, preferred_element_type=F32)
                target[:, span] = (
                    piece.astype(F32) * cosine[...] + turned * sine[...]
                ).astype(BF16)

    def back_copy(step):
        peer = lax.rem(slot + step, frame_size)
        return pltpu.make_async_remote_copy(
            src_ref=staged.at[peer],
            dst_ref=landed.at[:, mine],
            send_sem=back_send.at[peer],
            recv_sem=back_recv.at[slot],
            device_id=(me, peer),
            device_id_type=pl.DeviceIdType.MESH,
        )

    def back_arrival(step):
        peer = lax.rem(slot + step, frame_size)
        return pltpu.make_async_remote_copy(
            src_ref=staged.at[peer],
            dst_ref=landed.at[:, pl.ds(pl.multiple_of(peer * share, 16), share)],
            send_sem=back_send.at[peer],
            recv_sem=back_recv.at[peer],
            device_id=(me, peer),
            device_id_type=pl.DeviceIdType.MESH,
        )

    def finish(step, carry):
        peer = lax.rem(slot + step, frame_size)
        rows = pl.ds(pl.multiple_of(peer * chunk, 16), chunk)
        parts = []
        for pair in range(heads):
            span = slice(pair * PAIR, (pair + 1) * PAIR)
            parts.append(attend(tquery[rows, span], tkeys[:, span], tvalues[:, span], same[...]))
        time_mix = jnp.concatenate(parts, axis=1)
        before = gathered[pl.ds(peer * frames_dev, frames_dev)].reshape(chunk, width)
        after = (
            before.astype(F32) + jnp.dot(time_mix, tout[...], preferred_element_type=F32)
        ).astype(BF16)
        staged[peer] = after.reshape(frames_dev, share, width)

        @pl.when(step < frame_size)
        def _():
            back_copy(step).start()

        return carry

    lax.fori_loop(1, frame_size + 1, finish, 0)
    landed[:, mine] = staged[slot]
    for step in range(1, frame_size):
        back_arrival(step).wait_recv()
    out_ref[...] = landed[...]

    for f in range(frames_dev):
        to_mate(f).wait_send()

        @pl.when(has_above)
        def _():
            to_above(f).wait_send()

        @pl.when(has_below)
        def _():
            to_below(f).wait_send()

        @pl.when(gives_far)
        def _():
            hand_on(f).wait_send()

        for step in range(1, frame_size):
            frame_copy(f, step).wait_send()
    for step in range(1, frame_size):
        back_copy(step).wait_send()


def solution(mesh):
    res_size, frame_size = mesh.shape["res"], mesh.shape["frame"]

    def shards(activations, contacts, frame_index, spatial_qkv, spatial_out, time_qkv, time_out):
        frames_dev, block, width = activations.shape
        share = block // frame_size
        frames = frames_dev * frame_size
        size = frames * share
        vmem = pl.BlockSpec(memory_space=pltpu.VMEM)
        smem = pl.BlockSpec(memory_space=pltpu.SMEM)
        hbm = pl.BlockSpec(memory_space=pl.ANY)
        dma = pltpu.SemaphoreType.DMA
        return pl.pallas_call(
            functools.partial(kernel, res_size, frame_size),
            out_shape=jax.ShapeDtypeStruct((frames_dev, block, width), BF16),
            in_specs=[vmem, smem, smem, hbm, hbm, hbm, hbm],
            out_specs=vmem,
            scratch_shapes=[
                pltpu.VMEM(spatial_qkv.shape, BF16),
                pltpu.VMEM(spatial_out.shape, BF16),
                pltpu.VMEM(time_qkv.shape, BF16),
                pltpu.VMEM(time_out.shape, BF16),
                pltpu.VMEM((frames_dev, 5, block, width), BF16),
                pltpu.VMEM((frames_dev, block, width), BF16),
                pltpu.VMEM((frames_dev, 5 * block, width), BF16),
                pltpu.VMEM((frames_dev, 5 * block, width), BF16),
                pltpu.VMEM((block, width), BF16),
                pltpu.VMEM((frames_dev, block, width), BF16),
                pltpu.VMEM((frames, share, width), BF16),
                pltpu.VMEM((frame_size, frames_dev, share, width), BF16),
                pltpu.VMEM((frames_dev, block, width), BF16),
                pltpu.VMEM((size, width), BF16),
                pltpu.VMEM((size, width), BF16),
                pltpu.VMEM((size, width), BF16),
                pltpu.VMEM((size, PAIR), F32),
                pltpu.VMEM((size, PAIR), F32),
                pltpu.VMEM((2 * frames_dev * share, size), F32),
                dma((4,)),
                dma((frames_dev, 5)),
                dma((frames_dev, 5)),
                dma((frames_dev, frame_size)),
                dma((frames_dev, frame_size)),
                dma((frame_size,)),
                dma((frame_size,)),
            ],
            compiler_params=pltpu.CompilerParams(
                collective_id=0, has_side_effects=True, vmem_limit_bytes=48 * 1024 * 1024
            ),
        )(activations, contacts, frame_index, spatial_qkv, spatial_out, time_qkv, time_out)

    placed = (P("frame", "res", None), P(), P(), P(), P(), P(), P())
    return jax.shard_map(
        shards, mesh=mesh, in_specs=placed, out_specs=P("frame", "res", None), check_vma=False
    )
```

time: 212 us -> 52.7 us (0.25)
  the two profiles are of different devices: /device:TPU:3 before, /device:TPU:0 now
where the time goes in v1:
time: 52.7 us; the launch traced here: 52.4 us
  Pallas kernels  46.8 us (89%)
  local copies, waits for them, and re-layouts  5.62 us (11%)
    pallas_call x1, Pallas kernels, shards(): pl.pallas_call(functools.partial(kernel, res_size, frame_size), out_shape...  46.8 us
    unnamed x11, local copies, waits for them, and re-layouts  5.62 us

profile of v1, /device:TPU:0, one launch (start us, length us, event | category | flops | bytes accessed | tf_op | source)
XLA Modules:
  0.0 52.4 jit_solution(15573471952002134856)
XLA Ops:
  0.0 0.0 copy-start
  0.0 1.3 %copy-done = bf16[768,768]{1,0:T(8,128)(2,1)S(1)} copy-done((bf16[768,768]{1,0:T(8,128)(2,1)S(1)}, bf16[768,768]{1,0:T(8,128)(2,1)}, u32[]{:S(2)}) %copy-start) | copy-done | bytes 1179672
  1.3 0.0 copy-start.1
  1.3 1.3 %copy-done.1 = bf16[768,768]{1,0:T(8,128)(2,1)S(1)} copy-done((bf16[768,768]{1,0:T(8,128)(2,1)S(1)}, bf16[768,768]{1,0:T(8,128)(2,1)}, u32[]{:S(2)}) %copy-start.1) | copy-done | bytes 1179672
  2.5 0.0 copy-start.2
  2.5 1.0 %copy-done.2 = bf16[2,128,768]{2,1,0:T(8,128)(2,1)S(1)} copy-done((bf16[2,128,768]{2,1,0:T(8,128)(2,1)S(1)}, bf16[2,128,768]{2,1,0:T(8,128)(2,1)}, u32[]{:S(2)}) %copy-start.2) | copy-done | bytes 393240
  3.5 0.0 copy-start.3
  3.5 0.7 %copy-done.3 = s32[8,5]{1,0:T(8,128)S(1)} copy-done((s32[8,5]{1,0:T(8,128)S(1)}, s32[8,5]{1,0:T(8,128)}, u32[]{:S(2)}) %copy-start.3) | copy-done | bytes 184
  4.2 0.0 copy-start.4
  4.2 0.7 %copy-done.4 = s32[8]{0:T(128)S(1)} copy-done((s32[8]{0:T(128)S(1)}, s32[8]{0:T(128)}, u32[]{:S(2)}) %copy-start.4) | copy-done | bytes 56
  4.9 46.8 %shard_map.73 = bf16[2,128,768]{2,1,0:T(8,128)(2,1)S(1)} custom-call(bf16[2,128,768]{2,1,0:T(8,128)(2,1)S(1)} %copy-done.2, s32[8,5]{1,0:T(8,128)S(1)} %copy-done.3, s32[8]{0:T(128)S(1)} %copy-done.4, bf16[768,2304]{1,0:T(8,128)(2,1)} %sqkv_in.1, bf16[768,768]{1,0:T(8,128)(2,1)S(1)} %copy-done, bf16[768,2304]{1,0:T(8,128)(2,1)} %tqkv_in.1, ...), custom_call_target="tpu_custom_call" | custom-call | tf_op jit(solution)/shard_map/pallas_call | solution.py:345
  51.7 0.7 %copy.9 = bf16[2,128,768]{2,1,0:T(8,128)(2,1)} copy(bf16[2,128,768]{2,1,0:T(8,128)(2,1)S(1)} %shard_map.73) | data formatting | bytes 786432
Async XLA Ops:
  0.0 1.3 %copy-start = (bf16[768,768]{1,0:T(8,128)(2,1)S(1)}, bf16[768,768]{1,0:T(8,128)(2,1)}, u32[]{:S(2)}) copy-start(bf16[768,768]{1,0:T(8,128)(2,1)} %sout_in.1) | copy-start | bytes 3538948
  1.3 1.3 %copy-start.1 = (bf16[768,768]{1,0:T(8,128)(2,1)S(1)}, bf16[768,768]{1,0:T(8,128)(2,1)}, u32[]{:S(2)}) copy-start(bf16[768,768]{1,0:T(8,128)(2,1)} %tout_in.1) | copy-start | bytes 3538948
  2.5 1.0 %copy-start.2 = (bf16[2,128,768]{2,1,0:T(8,128)(2,1)S(1)}, bf16[2,128,768]{2,1,0:T(8,128)(2,1)}, u32[]{:S(2)}) copy-start(bf16[2,128,768]{2,1,0:T(8,128)(2,1)} %acts.1) | copy-start | bytes 1179652
  3.5 0.7 %copy-start.3 = (s32[8,5]{1,0:T(8,128)S(1)}, s32[8,5]{1,0:T(8,128)}, u32[]{:S(2)}) copy-start(s32[8,5]{1,0:T(8,128)} %contacts.1) | copy-start | bytes 484
  4.2 0.7 %copy-start.4 = (s32[8]{0:T(128)S(1)}, s32[8]{0:T(128)}, u32[]{:S(2)}) copy-start(s32[8]{0:T(128)} %frame_index.1) | copy-start | bytes 100

commit v2 on v1

--- a/solution.py
+++ b/solution.py
@@ -11,9 +11,14 @@
 HEAD = 64
 HALO = 2
 PAIR = 2 * HEAD
-OWN, NEAR, BELOW, ABOVE, FAR = range(5)
+OWN, NEAR, DIRECT, RELAYED, FAR = range(5)
 F32 = jnp.float32
 BF16 = jnp.bfloat16
+
+
+def exclusive(first, second, size):
+    bits = [1 << i for i in range(size.bit_length() - 1)]
+    return sum(((first // w + second // w) % 2) * w for w in bits)
 
 
 def normalize(values_in):
@@ -43,8 +48,8 @@
 
 def kernel(
     res_size, frame_size,
-    acts, contacts, frame_index, sqkv_in, sout_in, tqkv_in, tout_in, out_ref,
-    sqkv, sout, tqkv, tout, near, query, keys, values, mix, hidden, gathered, staged, landed,
+    acts_in, contacts, frame_index, sqkv_in, sout_in, tqkv_in, tout_in, out_ref,
+    acts, sqkv, sout, tqkv, tout, near, query, keys, values, mix, hidden, gathered, staged, landed,
     tquery, tkeys, tvalues, cosine, sine, same,
     weight_sem, halo_send, halo_recv, frame_send, frame_recv, back_send, back_recv,
 ):
@@ -56,11 +61,16 @@
     me = lax.axis_index("res")
     slot = lax.axis_index("frame")
     odd = lax.rem(me, 2)
+    side = lax.rem(me // 2, 2)
     mate = me + 1 - 2 * odd
-    has_below = me >= HALO
-    has_above = me < res_size - HALO
-    has_far = jnp.where(odd == 1, me + 1 < res_size, me >= 1)
-    gives_far = jnp.where(odd == 1, has_below, has_above)
+    across = me + 2 - 4 * side
+    relay_target = me + 4 - 8 * side
+    relay_source = me - 4 + 8 * side
+    gives_relay = jnp.logical_and(relay_target >= 0, relay_target < res_size)
+    has_relayed = jnp.logical_and(relay_source >= 0, relay_source < res_size)
+    gives_direct = side == odd
+    gives_relayed = jnp.logical_and(side != odd, has_relayed)
+    has_far = jnp.logical_or(side != odd, has_relayed)
 
     weights = [
         pltpu.make_async_copy(source, target, weight_sem.at[i])
@@ -68,6 +78,8 @@
             [(sqkv_in, sqkv), (sout_in, sout), (tqkv_in, tqkv), (tout_in, tout)]
         )
     ]
+    fetch = pltpu.make_async_copy(acts_in, acts, weight_sem.at[4])
+    fetch.start()
     for copy in weights:
         copy.start()
 
@@ -79,23 +91,25 @@
         )
 
     greet(mate, slot)
-
-    @pl.when(has_below)
+    greet(across, slot)
+
+    @pl.when(gives_relay)
     def _():
-        greet(me - HALO, slot)
-
-    @pl.when(has_above)
+        greet(relay_target, slot)
+
+    @pl.when(has_relayed)
     def _():
-        greet(me + HALO, slot)
+        greet(relay_source, slot)
 
     for step in range(1, frame_size):
-        greet(me, lax.rem(slot + step, frame_size))
-
+        greet(me, exclusive(slot, step, frame_size))
+
+    fetch.wait()
     for f in range(frames_dev):
         near[f, OWN] = normalize(acts[f])
 
     pl.semaphore_wait(
-        barrier, frame_size + has_below.astype(jnp.int32) + has_above.astype(jnp.int32)
+        barrier, frame_size + 1 + gives_relay.astype(jnp.int32) + has_relayed.astype(jnp.int32)
     )
 
     def halo(f, source, target, place):
@@ -111,28 +125,20 @@
     def to_mate(f):
         return halo(f, OWN, mate, NEAR)
 
-    def to_above(f):
-        return halo(f, OWN, me + HALO, BELOW)
-
-    def to_below(f):
-        return halo(f, OWN, me - HALO, ABOVE)
+    def to_across(f):
+        return halo(f, OWN, across, DIRECT)
+
+    def relay(f):
+        return halo(f, DIRECT, relay_target, RELAYED)
 
     def hand_on(f):
-        return halo(f, ABOVE - odd, mate, FAR)
-
-    for f in range(frames_dev):
-
-        @pl.when(has_above)
-        def _():
-            to_above(f).start()
-
-        @pl.when(has_below)
-        def _():
-            to_below(f).start()
-
+        return halo(f, DIRECT + side + odd - 2 * side * odd, mate, FAR)
+
+    for f in range(frames_dev):
+        to_across(f).start()
         to_mate(f).start()
 
-    for place, there in ((BELOW, has_below), (ABOVE, has_above), (FAR, has_far)):
+    for place, there in ((RELAYED, has_relayed), (FAR, has_far)):
 
         @pl.when(jnp.logical_not(there))
         def _():
@@ -161,7 +167,7 @@
         jnp.where(row == column - HEAD // 2, 1.0, 0.0),
         jnp.where(row == column + HEAD // 2, -1.0, 0.0),
     ).astype(BF16)
-    order = (HALO, 3 - 2 * odd, 0, 2 * HALO, 1 + 2 * odd)
+    order = (HALO, 3 - 2 * odd, 2 * HALO * (1 - side), 2 * HALO * side, 1 + 2 * odd)
     bias = jnp.concatenate(
         [
             jnp.full((1, block), jnp.where(contacts[me, place] > 0, 0.0, -1e30), F32)
@@ -178,14 +184,31 @@
                 rows, sqkv[:, part * width : (part + 1) * width], preferred_element_type=F32
             ).astype(BF16)
 
+    def pass_on(f):
+        to_across(f).wait_recv()
+
+        @pl.when(gives_relay)
+        def _():
+            relay(f).start()
+
+        @pl.when(gives_direct)
+        def _():
+            hand_on(f).start()
+
     weights[0].wait()
     for f in range(frames_dev):
         query[f] = jnp.dot(near[f, OWN], sqkv[:, :width], preferred_element_type=F32).astype(BF16)
         to_mate(f).wait_recv()
         project(f, OWN, 2)
+        if f == 0:
+            pass_on(0)
+    project(0, DIRECT, 1)
+    for f in range(1, frames_dev):
+        pass_on(f)
+        project(f, DIRECT, 1)
 
     def frame_copy(f, step):
-        peer = lax.rem(slot + step, frame_size)
+        peer = exclusive(slot, step, frame_size)
         return pltpu.make_async_remote_copy(
             src_ref=hidden.at[f, pl.ds(pl.multiple_of(peer * share, 16), share)],
             dst_ref=gathered.at[slot * frames_dev + f],
@@ -196,7 +219,7 @@
         )
 
     def frame_arrival(f, step):
-        peer = lax.rem(slot + step, frame_size)
+        peer = exclusive(slot, step, frame_size)
         return pltpu.make_async_remote_copy(
             src_ref=hidden.at[f, pl.ds(0, share)],
             dst_ref=gathered.at[peer * frames_dev + f],
@@ -209,19 +232,15 @@
     mine = pl.ds(pl.multiple_of(slot * share, 16), share)
     for f in range(frames_dev):
 
-        @pl.when(has_below)
-        def _():
-            to_above(f).wait_recv()
-
-        @pl.when(has_above)
-        def _():
-            to_below(f).wait_recv()
-
-        @pl.when(gives_far)
+        @pl.when(has_relayed)
+        def _():
+            relay(f).wait_recv()
+
+        @pl.when(gives_relayed)
         def _():
             hand_on(f).start()
 
-        project(f, BELOW, 2)
+        project(f, RELAYED, 1)
 
         @pl.when(has_far)
         def _():
@@ -262,7 +281,7 @@
                 ).astype(BF16)
 
     def back_copy(step):
-        peer = lax.rem(slot + step, frame_size)
+        peer = exclusive(slot, step, frame_size)
         return pltpu.make_async_remote_copy(
             src_ref=staged.at[peer],
             dst_ref=landed.at[:, mine],
@@ -273,7 +292,7 @@
         )
 
     def back_arrival(step):
-        peer = lax.rem(slot + step, frame_size)
+        peer = exclusive(slot, step, frame_size)
         return pltpu.make_async_remote_copy(
             src_ref=staged.at[peer],
             dst_ref=landed.at[:, pl.ds(pl.multiple_of(peer * share, 16), share)],
@@ -283,8 +302,9 @@
             device_id_type=pl.DeviceIdType.MESH,
         )
 
-    def finish(step, carry):
-        peer = lax.rem(slot + step, frame_size)
+    def finish(turn_at, carry):
+        step = frame_size - 1 - turn_at
+        peer = exclusive(slot, step, frame_size)
         rows = pl.ds(pl.multiple_of(peer * chunk, 16), chunk)
         parts = []
         for pair in range(heads):
@@ -297,13 +317,13 @@
         ).astype(BF16)
         staged[peer] = after.reshape(frames_dev, share, width)
 
-        @pl.when(step < frame_size)
+        @pl.when(step > 0)
         def _():
             back_copy(step).start()
 
         return carry
 
-    lax.fori_loop(1, frame_size + 1, finish, 0)
+    lax.fori_loop(0, frame_size, finish, 0)
     landed[:, mine] = staged[slot]
     for step in range(1, frame_size):
         back_arrival(step).wait_recv()
@@ -312,15 +332,13 @@
     for f in range(frames_dev):
         to_mate(f).wait_send()
 
-        @pl.when(has_above)
-        def _():
-            to_above(f).wait_send()
-
-        @pl.when(has_below)
-        def _():
-            to_below(f).wait_send()
-
-        @pl.when(gives_far)
+        to_across(f).wait_send()
+
+        @pl.when(gives_relay)
+        def _():
+            relay(f).wait_send()
+
+        @pl.when(jnp.logical_or(gives_direct, gives_relayed))
         def _():
             hand_on(f).wait_send()
 
@@ -340,14 +358,15 @@
         size = frames * share
         vmem = pl.BlockSpec(memory_space=pltpu.VMEM)
         smem = pl.BlockSpec(memory_space=pltpu.SMEM)
-        hbm = pl.BlockSpec(memory_space=pl.ANY)
+        hbm = pl.BlockSpec(memory_space=pltpu.HBM)
         dma = pltpu.SemaphoreType.DMA
         return pl.pallas_call(
             functools.partial(kernel, res_size, frame_size),
             out_shape=jax.ShapeDtypeStruct((frames_dev, block, width), BF16),
-            in_specs=[vmem, smem, smem, hbm, hbm, hbm, hbm],
+            in_specs=[hbm, smem, smem, hbm, hbm, hbm, hbm],
             out_specs=vmem,
             scratch_shapes=[
+                pltpu.VMEM((frames_dev, block, width), BF16),
                 pltpu.VMEM(spatial_qkv.shape, BF16),
                 pltpu.VMEM(spatial_out.shape, BF16),
                 pltpu.VMEM(time_qkv.shape, BF16),
@@ -367,7 +386,7 @@
                 pltpu.VMEM((size, PAIR), F32),
                 pltpu.VMEM((size, PAIR), F32),
                 pltpu.VMEM((2 * frames_dev * share, size), F32),
-                dma((4,)),
+                dma((5,)),
                 dma((frames_dev, 5)),
                 dma((frames_dev, 5)),
                 dma((frames_dev, frame_size)),
@@ -376,7 +395,7 @@
                 dma((frame_size,)),
             ],
             compiler_params=pltpu.CompilerParams(
-                collective_id=0, has_side_effects=True, vmem_limit_bytes=48 * 1024 * 1024
+                collective_id=0, has_side_effects=True, vmem_limit_bytes=56 * 1024 * 1024
             ),
         )(activations, contacts, frame_index, spatial_qkv, spatial_out, time_qkv, time_out)
 

time: 52.7 us -> 46.9 us (0.89)
  the two profiles are of different devices: /device:TPU:0 before, /device:TPU:3 now
where the time goes in v2:
time: 46.9 us; the launch traced here: 46.7 us
  Pallas kernels  44.9 us (96%)
  local copies, waits for them, and re-layouts  1.77 us (4%)
    pallas_call x1, Pallas kernels, shards(): pl.pallas_call(functools.partial(kernel, res_size, frame_size), out_shape...  44.9 us
    unnamed x1, local copies, waits for them, and re-layouts  1.77 us

profile of v2, /device:TPU:3, one launch (start us, length us, event | category | flops | bytes accessed | tf_op | source)
XLA Modules:
  0.0 46.7 jit_solution(2276016524305338385)
XLA Ops:
  0.0 44.9 %shard_map.73 = bf16[2,128,768]{2,1,0:T(8,128)(2,1)} custom-call(bf16[2,128,768]{2,1,0:T(8,128)(2,1)} %acts_in.1, s32[8,5]{1,0:T(8,128)} %contacts.1, s32[8]{0:T(128)} %frame_index.1, bf16[768,2304]{1,0:T(8,128)(2,1)} %sqkv_in.1, bf16[768,768]{1,0:T(8,128)(2,1)} %sout_in.1, bf16[768,2304]{1,0:T(8,128)(2,1)} %tqkv_in.1, bf16[768,768]{1,0:T(8,128)(2,1)} %tout_in.1), custom_call_target="tpu_custom_call" | custom-call | tf_op jit(solution)/shard_map/pallas_call | solution.py:363
  44.9 1.8 %copy.9 = bf16[2,128,768]{2,1,0:T(8,128)(2,1)} copy(bf16[2,128,768]{2,1,0:T(8,128)(2,1)} %shard_map.73) | data formatting | bytes 786432

commit v3 on v2

v3 whole, which is shorter than its diff:
```python
import functools
import math

import jax
import jax.numpy as jnp
from jax import lax
from jax.experimental import pallas as pl
from jax.experimental.pallas import tpu as pltpu
from jax.sharding import PartitionSpec as P

HEAD = 64
HALO = 2
PAIR = 2 * HEAD
OWN, NEAR, DIRECT, RELAYED, FAR = range(5)
F32 = jnp.float32
BF16 = jnp.bfloat16


def exclusive(first, second, size):
    bits = [1 << i for i in range(size.bit_length() - 1)]
    return sum(((first // w + second // w) % 2) * w for w in bits)


def normalize(values_in):
    widened = values_in.astype(F32)
    mean_square = jnp.mean(widened * widened, axis=-1, keepdims=True)
    return (widened * lax.rsqrt(mean_square + 1e-06)).astype(BF16)


def attend(query, keys, values, bias):
    rows = query.shape[0]
    lanes = lax.broadcasted_iota(jnp.int32, (1, PAIR), 1)
    first = jnp.where(lanes < HEAD, HEAD ** (-0.5), 0.0).astype(BF16)
    second = jnp.where(lanes < HEAD, 0.0, HEAD ** (-0.5)).astype(BF16)
    both = jnp.concatenate([query * first, query * second], axis=0)
    scores = (
        lax.dot_general(both, keys, (((1,), (1,)), ((), ())), preferred_element_type=F32) + bias
    )
    top = jnp.max(scores, axis=-1, keepdims=True)
    expo = jnp.exp(scores - top).astype(BF16)
    wide = jnp.concatenate([values, jnp.ones_like(values)], axis=1)
    mixed = jnp.dot(expo, wide, preferred_element_type=F32)
    low = lax.broadcasted_iota(jnp.int32, (rows, PAIR), 1) < HEAD
    total = jnp.where(low, mixed[:rows, :PAIR], mixed[rows:, :PAIR])
    count = jnp.where(low, mixed[:rows, PAIR:], mixed[rows:, PAIR:])
    return (total / count).astype(BF16)


def kernel(
    res_size, frame_size,
    acts_in, contacts, frame_index, sqkv_in, sout_in, tqkv_in, tout_in, out_ref,
    acts, sqkv, sout, tqkv, tout, near, query, keys, values, mix, hidden, gathered, staged, landed,
    tquery, tkeys, tvalues, cosine, sine, same,
    weight_sem, halo_send, halo_recv, frame_send, frame_recv, back_send, back_recv,
):
    frames_dev, block, width = acts.shape
    heads = width // PAIR
    parts, share, halves = gathered.shape[0], gathered.shape[2], halo_send.shape[2]
    frames = frames_dev * frame_size
    chunk = frames_dev * share
    me = lax.axis_index("res")
    slot = lax.axis_index("frame")
    odd = lax.rem(me, 2)
    side = lax.rem(me // 2, 2)
    mate = me + 1 - 2 * odd
    across = me + 2 - 4 * side
    relay_target = me + 4 - 8 * side
    relay_source = me - 4 + 8 * side
    gives_relay = jnp.logical_and(relay_target >= 0, relay_target < res_size)
    has_relayed = jnp.logical_and(relay_source >= 0, relay_source < res_size)
    gives_direct = side == odd
    gives_relayed = jnp.logical_and(side != odd, has_relayed)
    has_far = jnp.logical_or(side != odd, has_relayed)

    weights = [
        pltpu.make_async_copy(source, target, weight_sem.at[i])
        for i, (source, target) in enumerate(
            [(sqkv_in, sqkv), (sout_in, sout), (tqkv_in, tqkv), (tout_in, tout)]
        )
    ]
    fetch = pltpu.make_async_copy(acts_in, acts, weight_sem.at[4])
    fetch.start()
    for copy in weights:
        copy.start()

    barrier = pltpu.get_barrier_semaphore()

    def greet(res, frame):
        pl.semaphore_signal(
            barrier, inc=1, device_id=(res, frame), device_id_type=pl.DeviceIdType.MESH
        )

    greet(mate, slot)
    greet(across, slot)

    @pl.when(gives_relay)
    def _():
        greet(relay_target, slot)

    @pl.when(has_relayed)
    def _():
        greet(relay_source, slot)

    for step in range(1, frame_size):
        greet(me, exclusive(slot, step, frame_size))

    fetch.wait()
    for f in range(frames_dev):
        near[f, OWN] = normalize(acts[f])

    pl.semaphore_wait(
        barrier, frame_size + 1 + gives_relay.astype(jnp.int32) + has_relayed.astype(jnp.int32)
    )

    def halo(f, half, source, target, place):
        rows = pl.ds(half * (block // halves), block // halves)
        return pltpu.make_async_remote_copy(
            src_ref=near.at[f, source, rows],
            dst_ref=near.at[f, place, rows],
            send_sem=halo_send.at[f, place, half],
            recv_sem=halo_recv.at[f, place, half],
            device_id=(target, slot),
            device_id_type=pl.DeviceIdType.MESH,
        )

    def to_mate(f, half):
        return halo(f, half, OWN, mate, NEAR)

    def to_across(f, half):
        return halo(f, half, OWN, across, DIRECT)

    def relay(f, half):
        return halo(f, half, DIRECT, relay_target, RELAYED)

    def hand_on(f, half):
        return halo(f, half, DIRECT + side + odd - 2 * side * odd, mate, FAR)

    for f in range(frames_dev):
        for half in range(halves):
            to_across(f, half).start()
            to_mate(f, half).start()

    for place, there in ((RELAYED, has_relayed), (FAR, has_far)):

        @pl.when(jnp.logical_not(there))
        def _():
            near[:, place] = jnp.zeros((frames_dev, block, width), BF16)

    size = frames * share
    lane = lax.broadcasted_iota(jnp.int32, (frames, PAIR), 1)
    row = lax.broadcasted_iota(jnp.int32, (frames, PAIR), 0)
    frequency = jnp.exp((lane & (HEAD // 2 - 1)).astype(F32) * (-math.log(10000.0) / (HEAD // 2)))
    position = jnp.zeros((frames, PAIR), F32)
    for g in range(frames):
        position = jnp.where(row == g, frame_index[g].astype(F32), position)
    angle = position * frequency
    for table, entries in ((cosine, jnp.cos(angle)), (sine, jnp.sin(angle))):
        table[...] = jnp.broadcast_to(entries[:, None, :], (frames, share, PAIR)).reshape(
            size, PAIR
        )
    row = lax.broadcasted_iota(jnp.int32, same.shape, 0)
    column = lax.broadcasted_iota(jnp.int32, same.shape, 1)
    same[...] = jnp.where((row & (share - 1)) == (column & (share - 1)), 0.0, -1e30)
    row = lax.broadcasted_iota(jnp.int32, (PAIR, PAIR), 0)
    column = lax.broadcasted_iota(jnp.int32, (PAIR, PAIR), 1)
    upper = (column & (HEAD - 1)) >= HEAD // 2
    turn = jnp.where(
        upper,
        jnp.where(row == column - HEAD // 2, 1.0, 0.0),
        jnp.where(row == column + HEAD // 2, -1.0, 0.0),
    ).astype(BF16)
    order = (HALO, 3 - 2 * odd, 2 * HALO * (1 - side), 2 * HALO * side, 1 + 2 * odd)
    bias = jnp.concatenate(
        [
            jnp.full((1, block), jnp.where(contacts[me, place] > 0, 0.0, -1e30), F32)
            for place in order
        ],
        axis=1,
    )

    def project(f, first, count):
        rows = near[f, first : first + count].reshape(count * block, width)
        span = slice(first * block, (first + count) * block)
        for part, target in ((1, keys), (2, values)):
            target[f, span] = jnp.dot(
                rows, sqkv[:, part * width : (part + 1) * width], preferred_element_type=F32
            ).astype(BF16)

    def pass_on(f, half):
        to_across(f, half).wait_recv()

        @pl.when(gives_relay)
        def _():
            relay(f, half).start()

        @pl.when(gives_direct)
        def _():
            hand_on(f, half).start()

    def take_relayed(f):
        for half in range(halves):

            @pl.when(has_relayed)
            def _():
                relay(f, half).wait_recv()

            @pl.when(gives_relayed)
            def _():
                hand_on(f, half).start()

        project(f, RELAYED, 1)

    def take_far(f):
        @pl.when(has_far)
        def _():
            for half in range(halves):
                hand_on(f, half).wait_recv()

        project(f, FAR, 1)

    def frame_copy(f, part, step):
        peer = exclusive(slot, step, frame_size)
        first = part * (block // parts) + peer * share
        return pltpu.make_async_remote_copy(
            src_ref=hidden.at[f, pl.ds(pl.multiple_of(first, 16), share)],
            dst_ref=gathered.at[part, slot * frames_dev + f],
            send_sem=frame_send.at[f, part, peer],
            recv_sem=frame_recv.at[f, part, slot],
            device_id=(me, peer),
            device_id_type=pl.DeviceIdType.MESH,
        )

    def frame_arrival(f, part, step):
        peer = exclusive(slot, step, frame_size)
        return pltpu.make_async_remote_copy(
            src_ref=hidden.at[f, pl.ds(0, share)],
            dst_ref=gathered.at[part, peer * frames_dev + f],
            send_sem=frame_send.at[f, part, peer],
            recv_sem=frame_recv.at[f, part, peer],
            device_id=(me, peer),
            device_id_type=pl.DeviceIdType.MESH,
        )

    def spatial(f, first, count):
        rows = slice(first * (block // parts), (first + count) * (block // parts))
        for pair in range(heads):
            span = slice(pair * PAIR, (pair + 1) * PAIR)
            mix[rows, span] = attend(
                query[f, rows, span], keys[f, :, span], values[f, :, span], bias
            )
        hidden[f, rows] = (
            acts[f, rows].astype(F32)
            + jnp.dot(mix[rows], sout[...], preferred_element_type=F32)
        ).astype(BF16)
        for part in range(first, first + count):
            for step in range(frame_size - 1, 0, -1):
                frame_copy(f, part, step).start()
            mine = pl.ds(pl.multiple_of(part * (block // parts) + slot * share, 16), share)
            gathered[part, slot * frames_dev + f] = hidden[f, mine]

    weights[0].wait()
    for f in range(frames_dev):
        query[f] = jnp.dot(near[f, OWN], sqkv[:, :width], preferred_element_type=F32).astype(BF16)
        for half in range(halves):
            to_mate(f, half).wait_recv()
        project(f, OWN, 2)
        pass_on(0, f)
    project(0, DIRECT, 1)
    pass_on(1, 0)
    take_relayed(0)
    pass_on(1, 1)
    take_far(0)
    weights[1].wait()
    spatial(0, 0, parts)
    project(1, DIRECT, 1)
    take_relayed(1)
    take_far(1)
    for part in range(parts):
        spatial(1, part, 1)

    def back_copy(part, peer):
        first = part * (block // parts) + slot * share
        return pltpu.make_async_remote_copy(
            src_ref=staged.at[part, peer],
            dst_ref=landed.at[:, pl.ds(pl.multiple_of(first, 16), share)],
            send_sem=back_send.at[part, peer],
            recv_sem=back_recv.at[part, slot],
            device_id=(me, peer),
            device_id_type=pl.DeviceIdType.MESH,
        )

    def back_arrival(part, peer):
        first = part * (block // parts) + peer * share
        return pltpu.make_async_remote_copy(
            src_ref=staged.at[part, peer],
            dst_ref=landed.at[:, pl.ds(pl.multiple_of(first, 16), share)],
            send_sem=back_send.at[part, peer],
            recv_sem=back_recv.at[part, peer],
            device_id=(me, peer),
            device_id_type=pl.DeviceIdType.MESH,
        )

    weights[2].wait()
    weights[3].wait()
    for part in range(parts):
        for f in range(frames_dev):
            for step in range(1, frame_size):
                frame_arrival(f, part, step).wait_recv()
        renormed = normalize(gathered[part].reshape(size, width))
        for third, target in ((0, tquery), (1, tkeys), (2, tvalues)):
            projected = jnp.dot(
                renormed, tqkv[:, third * width : (third + 1) * width], preferred_element_type=F32
            ).astype(BF16)
            if third == 2:
                target[...] = projected
            else:
                for pair in range(heads):
                    span = slice(pair * PAIR, (pair + 1) * PAIR)
                    piece = projected[:, span]
                    turned = jnp.dot(piece, turn, preferred_element_type=F32)
                    target[:, span] = (
                        piece.astype(F32) * cosine[...] + turned * sine[...]
                    ).astype(BF16)
        for apart in range(frame_size // 2 - 1, -1, -1):
            first = 2 * exclusive(slot // 2, apart, frame_size // 2)
            rows = pl.ds(pl.multiple_of(first * chunk, 16), 2 * chunk)
            pieces = []
            for pair in range(heads):
                span = slice(pair * PAIR, (pair + 1) * PAIR)
                pieces.append(
                    attend(tquery[rows, span], tkeys[:, span], tvalues[:, span], same[...])
                )
            time_mix = jnp.concatenate(pieces, axis=1)
            before = gathered[part, pl.ds(first * frames_dev, 2 * frames_dev)]
            after = (
                before.reshape(2 * chunk, width).astype(F32)
                + jnp.dot(time_mix, tout[...], preferred_element_type=F32)
            ).astype(BF16)
            staged[part, pl.ds(first, 2)] = after.reshape(2, frames_dev, share, width)
            if apart > 0:
                back_copy(part, first).start()
                back_copy(part, first + 1).start()
            else:
                back_copy(part, first + 1 - slot % 2).start()
                mine = pl.ds(pl.multiple_of(part * (block // parts) + slot * share, 16), share)
                landed[:, mine] = staged[part, slot]

    for part in range(parts):
        for step in range(1, frame_size):
            back_arrival(part, exclusive(slot, step, frame_size)).wait_recv()
    out_ref[...] = landed[...]

    for f in range(frames_dev):
        for half in range(halves):
            to_mate(f, half).wait_send()
            to_across(f, half).wait_send()

            @pl.when(gives_relay)
            def _():
                relay(f, half).wait_send()

            @pl.when(jnp.logical_or(gives_direct, gives_relayed))
            def _():
                hand_on(f, half).wait_send()

        for part in range(parts):
            for step in range(1, frame_size):
                frame_copy(f, part, step).wait_send()
    for part in range(parts):
        for step in range(1, frame_size):
            back_copy(part, exclusive(slot, step, frame_size)).wait_send()


def solution(mesh):
    res_size, frame_size = mesh.shape["res"], mesh.shape["frame"]

    def shards(activations, contacts, frame_index, spatial_qkv, spatial_out, time_qkv, time_out):
        frames_dev, block, width = activations.shape
        share = 16
        parts = block // (frame_size * share)
        frames = frames_dev * frame_size
        size = frames * share
        vmem = pl.BlockSpec(memory_space=pltpu.VMEM)
        smem = pl.BlockSpec(memory_space=pltpu.SMEM)
        hbm = pl.BlockSpec(memory_space=pltpu.HBM)
        dma = pltpu.SemaphoreType.DMA
        return pl.pallas_call(
            functools.partial(kernel, res_size, frame_size),
            out_shape=jax.ShapeDtypeStruct((frames_dev, block, width), BF16),
            in_specs=[hbm, smem, smem, hbm, hbm, hbm, hbm],
            out_specs=vmem,
            scratch_shapes=[
                pltpu.VMEM((frames_dev, block, width), BF16),
                pltpu.VMEM(spatial_qkv.shape, BF16),
                pltpu.VMEM(spatial_out.shape, BF16),
                pltpu.VMEM(time_qkv.shape, BF16),
                pltpu.VMEM(time_out.shape, BF16),
                pltpu.VMEM((frames_dev, 5, block, width), BF16),
                pltpu.VMEM((frames_dev, block, width), BF16),
                pltpu.VMEM((frames_dev, 5 * block, width), BF16),
                pltpu.VMEM((frames_dev, 5 * block, width), BF16),
                pltpu.VMEM((block, width), BF16),
                pltpu.VMEM((frames_dev, block, width), BF16),
                pltpu.VMEM((parts, frames, share, width), BF16),
                pltpu.VMEM((parts, frame_size, frames_dev, share, width), BF16),
                pltpu.VMEM((frames_dev, block, width), BF16),
                pltpu.VMEM((size, width), BF16),
                pltpu.VMEM((size, width), BF16),
                pltpu.VMEM((size, width), BF16),
                pltpu.VMEM((size, PAIR), F32),
                pltpu.VMEM((size, PAIR), F32),
                pltpu.VMEM((4 * frames_dev * share, size), F32),
                dma((5,)),
                dma((frames_dev, 5, 2)),
                dma((frames_dev, 5, 2)),
                dma((frames_dev, parts, frame_size)),
                dma((frames_dev, parts, frame_size)),
                dma((parts, frame_size)),
                dma((parts, frame_size)),
            ],
            compiler_params=pltpu.CompilerParams(
                collective_id=0, has_side_effects=True, vmem_limit_bytes=53 * 1024 * 1024
            ),
        )(activations, contacts, frame_index, spatial_qkv, spatial_out, time_qkv, time_out)

    placed = (P("frame", "res", None), P(), P(), P(), P(), P(), P())
    return jax.shard_map(
        shards, mesh=mesh, in_specs=placed, out_specs=P("frame", "res", None), check_vma=False
    )
```

time: 46.9 us -> 43.4 us (0.925)
  Pallas kernels: 44.9 us -> 40.1 us
  local copies, waits for them, and re-layouts: 1.77 us -> 3.08 us
    pallas_call x1, Pallas kernels: 44.9 us -> 40.1 us  [shards(): pl.pallas_call(functools.partial(kernel, res_size, frame_size), out_shape...]
    unnamed x1 -> x7, local copies, waits for them, and re-layouts: 1.77 us -> 3.08 us
where the time goes in v3:
time: 43.4 us; the launch traced here: 43.2 us
  Pallas kernels  40.1 us (92%)
  local copies, waits for them, and re-layouts  3.08 us (7%)
    pallas_call x1, Pallas kernels, shards(): pl.pallas_call(functools.partial(kernel, res_size, frame_size), out_shape...  40.1 us
    unnamed x7, local copies, waits for them, and re-layouts  3.08 us

profile of v3, /device:TPU:3, one launch (start us, length us, event | category | flops | bytes accessed | tf_op | source)
XLA Modules:
  0.0 43.2 jit_solution(10117926679955497256)
XLA Ops:
  0.0 0.0 copy-start
  0.0 1.0 %copy-done = bf16[2,128,768]{2,1,0:T(8,128)(2,1)S(1)} copy-done((bf16[2,128,768]{2,1,0:T(8,128)(2,1)S(1)}, bf16[2,128,768]{2,1,0:T(8,128)(2,1)}, u32[]{:S(2)}) %copy-start) | copy-done | bytes 393240
  1.0 0.0 copy-start.1
  1.0 0.7 %copy-done.1 = s32[8,5]{1,0:T(8,128)S(1)} copy-done((s32[8,5]{1,0:T(8,128)S(1)}, s32[8,5]{1,0:T(8,128)}, u32[]{:S(2)}) %copy-start.1) | copy-done | bytes 184
  1.7 0.0 copy-start.2
  1.7 0.7 %copy-done.2 = s32[8]{0:T(128)S(1)} copy-done((s32[8]{0:T(128)S(1)}, s32[8]{0:T(128)}, u32[]{:S(2)}) %copy-start.2) | copy-done | bytes 56
  2.3 40.1 %shard_map.73 = bf16[2,128,768]{2,1,0:T(8,128)(2,1)S(1)} custom-call(bf16[2,128,768]{2,1,0:T(8,128)(2,1)S(1)} %copy-done, s32[8,5]{1,0:T(8,128)S(1)} %copy-done.1, s32[8]{0:T(128)S(1)} %copy-done.2, bf16[768,2304]{1,0:T(8,128)(2,1)} %sqkv_in.1, bf16[768,768]{1,0:T(8,128)(2,1)} %sout_in.1, bf16[768,2304]{1,0:T(8,128)(2,1)} %tqkv_in.1, bf16[768,768]{1,0:T(8,128)(2,1)} %tout_in.1), custom_call_target="tpu_custom_call" | custom-call | tf_op jit(solution)/shard_map/pallas_call | solution.py:387
  42.4 0.7 %copy.9 = bf16[2,128,768]{2,1,0:T(8,128)(2,1)} copy(bf16[2,128,768]{2,1,0:T(8,128)(2,1)S(1)} %shard_map.73) | data formatting | bytes 786432
Async XLA Ops:
  0.0 1.0 %copy-start = (bf16[2,128,768]{2,1,0:T(8,128)(2,1)S(1)}, bf16[2,128,768]{2,1,0:T(8,128)(2,1)}, u32[]{:S(2)}) copy-start(bf16[2,128,768]{2,1,0:T(8,128)(2,1)} %acts_in.1) | copy-start | bytes 1179652
  1.0 0.7 %copy-start.1 = (s32[8,5]{1,0:T(8,128)S(1)}, s32[8,5]{1,0:T(8,128)}, u32[]{:S(2)}) copy-start(s32[8,5]{1,0:T(8,128)} %contacts.1) | copy-start | bytes 484
  1.7 0.7 %copy-start.2 = (s32[8]{0:T(128)S(1)}, s32[8]{0:T(128)}, u32[]{:S(2)}) copy-start(s32[8]{0:T(128)} %frame_index.1) | copy-start | bytes 100

commit v4 on v3

--- a/solution.py
+++ b/solution.py
@@ -41,16 +41,17 @@
     wide = jnp.concatenate([values, jnp.ones_like(values)], axis=1)
     mixed = jnp.dot(expo, wide, preferred_element_type=F32)
     low = lax.broadcasted_iota(jnp.int32, (rows, PAIR), 1) < HEAD
+    highest = jnp.where(low, top[:rows], top[rows:])
     total = jnp.where(low, mixed[:rows, :PAIR], mixed[rows:, :PAIR])
     count = jnp.where(low, mixed[:rows, PAIR:], mixed[rows:, PAIR:])
-    return (total / count).astype(BF16)
+    return highest, total, count
 
 
 def kernel(
     res_size, frame_size,
     acts_in, contacts, frame_index, sqkv_in, sout_in, tqkv_in, tout_in, out_ref,
     acts, sqkv, sout, tqkv, tout, near, query, keys, values, mix, hidden, gathered, staged, landed,
-    tquery, tkeys, tvalues, cosine, sine, same,
+    tquery, tkeys, tvalues, cosine, sine, same, highest, total, count,
     weight_sem, halo_send, halo_recv, frame_send, frame_recv, back_send, back_recv,
 ):
     frames_dev, block, width = acts.shape
@@ -144,7 +145,10 @@
 
         @pl.when(jnp.logical_not(there))
         def _():
-            near[:, place] = jnp.zeros((frames_dev, block, width), BF16)
+            for target in (keys, values):
+                target[:, place * block : (place + 1) * block] = jnp.zeros(
+                    (frames_dev, block, width), BF16
+                )
 
     size = frames * share
     lane = lax.broadcasted_iota(jnp.int32, (frames, PAIR), 1)
@@ -208,15 +212,16 @@
             def _():
                 hand_on(f, half).start()
 
-        project(f, RELAYED, 1)
+        @pl.when(has_relayed)
+        def _():
+            project(f, RELAYED, 1)
 
     def take_far(f):
         @pl.when(has_far)
         def _():
             for half in range(halves):
                 hand_on(f, half).wait_recv()
-
-        project(f, FAR, 1)
+            project(f, FAR, 1)
 
     def frame_copy(f, part, step):
         peer = exclusive(slot, step, frame_size)
@@ -241,18 +246,38 @@
             device_id_type=pl.DeviceIdType.MESH,
         )
 
-    def spatial(f, first, count):
-        rows = slice(first * (block // parts), (first + count) * (block // parts))
+    split = RELAYED * block
+
+    def begin(f):
         for pair in range(heads):
             span = slice(pair * PAIR, (pair + 1) * PAIR)
-            mix[rows, span] = attend(
-                query[f, rows, span], keys[f, :, span], values[f, :, span], bias
+            highest[:, span], total[:, span], count[:, span] = attend(
+                query[f, :, span],
+                keys[f, :split, span],
+                values[f, :split, span],
+                bias[:, :split],
             )
+
+    def spatial(f, first, many):
+        rows = slice(first * (block // parts), (first + many) * (block // parts))
+        for pair in range(heads):
+            span = slice(pair * PAIR, (pair + 1) * PAIR)
+            top, more, extra = attend(
+                query[f, rows, span],
+                keys[f, split:, span],
+                values[f, split:, span],
+                bias[:, split:],
+            )
+            peak = jnp.maximum(highest[rows, span], top)
+            old, new = jnp.exp(highest[rows, span] - peak), jnp.exp(top - peak)
+            mix[rows, span] = (
+                (total[rows, span] * old + more * new) / (count[rows, span] * old + extra * new)
+            ).astype(BF16)
         hidden[f, rows] = (
             acts[f, rows].astype(F32)
             + jnp.dot(mix[rows], sout[...], preferred_element_type=F32)
         ).astype(BF16)
-        for part in range(first, first + count):
+        for part in range(first, first + many):
             for step in range(frame_size - 1, 0, -1):
                 frame_copy(f, part, step).start()
             mine = pl.ds(pl.multiple_of(part * (block // parts) + slot * share, 16), share)
@@ -266,6 +291,7 @@
         project(f, OWN, 2)
         pass_on(0, f)
     project(0, DIRECT, 1)
+    begin(0)
     pass_on(1, 0)
     take_relayed(0)
     pass_on(1, 1)
@@ -273,6 +299,7 @@
     weights[1].wait()
     spatial(0, 0, parts)
     project(1, DIRECT, 1)
+    begin(1)
     take_relayed(1)
     take_far(1)
     for part in range(parts):
@@ -327,9 +354,10 @@
             pieces = []
             for pair in range(heads):
                 span = slice(pair * PAIR, (pair + 1) * PAIR)
-                pieces.append(
-                    attend(tquery[rows, span], tkeys[:, span], tvalues[:, span], same[...])
+                _, time_total, time_count = attend(
+                    tquery[rows, span], tkeys[:, span], tvalues[:, span], same[...]
                 )
+                pieces.append((time_total / time_count).astype(BF16))
             time_mix = jnp.concatenate(pieces, axis=1)
             before = gathered[part, pl.ds(first * frames_dev, 2 * frames_dev)]
             after = (
@@ -410,6 +438,9 @@
                 pltpu.VMEM((size, PAIR), F32),
                 pltpu.VMEM((size, PAIR), F32),
                 pltpu.VMEM((4 * frames_dev * share, size), F32),
+                pltpu.VMEM((block, width), F32),
+                pltpu.VMEM((block, width), F32),
+                pltpu.VMEM((block, width), F32),
                 dma((5,)),
                 dma((frames_dev, 5, 2)),
                 dma((frames_dev, 5, 2)),
@@ -419,7 +450,7 @@
                 dma((parts, frame_size)),
             ],
             compiler_params=pltpu.CompilerParams(
-                collective_id=0, has_side_effects=True, vmem_limit_bytes=53 * 1024 * 1024
+                collective_id=0, has_side_effects=True, vmem_limit_bytes=56 * 1024 * 1024
             ),
         )(activations, contacts, frame_index, spatial_qkv, spatial_out, time_qkv, time_out)
 

time: 43.4 us -> 41.1 us (0.947)
  local copies, waits for them, and re-layouts: 3.08 us -> 1.77 us
  Pallas kernels: 40.1 us -> 39.1 us
    unnamed x7 -> x1, local copies, waits for them, and re-layouts: 3.08 us -> 1.77 us
    pallas_call x1, Pallas kernels: 40.1 us -> 39.1 us  [shards(): pl.pallas_call(functools.partial(kernel, res_size, frame_size), out_shape...]
where the time goes in v4:
time: 41.1 us; the launch traced here: 40.9 us
  Pallas kernels  39.1 us (95%)
  local copies, waits for them, and re-layouts  1.77 us (4%)
    pallas_call x1, Pallas kernels, shards(): pl.pallas_call(functools.partial(kernel, res_size, frame_size), out_shape...  39.1 us
    unnamed x1, local copies, waits for them, and re-layouts  1.77 us

profile of v4, /device:TPU:3, one launch (start us, length us, event | category | flops | bytes accessed | tf_op | source)
XLA Modules:
  0.0 40.9 jit_solution(10268971382845737068)
XLA Ops:
  0.0 39.1 %shard_map.73 = bf16[2,128,768]{2,1,0:T(8,128)(2,1)} custom-call(bf16[2,128,768]{2,1,0:T(8,128)(2,1)} %acts_in.1, s32[8,5]{1,0:T(8,128)} %contacts.1, s32[8]{0:T(128)} %frame_index.1, bf16[768,2304]{1,0:T(8,128)(2,1)} %sqkv_in.1, bf16[768,768]{1,0:T(8,128)(2,1)} %sout_in.1, bf16[768,2304]{1,0:T(8,128)(2,1)} %tqkv_in.1, bf16[768,768]{1,0:T(8,128)(2,1)} %tout_in.1), custom_call_target="tpu_custom_call" | custom-call | tf_op jit(solution)/shard_map/pallas_call | solution.py:415
  39.1 1.8 %copy.9 = bf16[2,128,768]{2,1,0:T(8,128)(2,1)} copy(bf16[2,128,768]{2,1,0:T(8,128)(2,1)} %shard_map.73) | data formatting | bytes 786432

commit v5 on v4

--- a/solution.py
+++ b/solution.py
@@ -56,7 +56,7 @@
 ):
     frames_dev, block, width = acts.shape
     heads = width // PAIR
-    parts, share, halves = gathered.shape[0], gathered.shape[2], halo_send.shape[2]
+    parts, share, halves = gathered.shape[1], gathered.shape[3], halo_send.shape[2]
     frames = frames_dev * frame_size
     chunk = frames_dev * share
     me = lax.axis_index("res")
@@ -81,8 +81,7 @@
     ]
     fetch = pltpu.make_async_copy(acts_in, acts, weight_sem.at[4])
     fetch.start()
-    for copy in weights:
-        copy.start()
+    weights[0].start()
 
     barrier = pltpu.get_barrier_semaphore()
 
@@ -106,8 +105,7 @@
         greet(me, exclusive(slot, step, frame_size))
 
     fetch.wait()
-    for f in range(frames_dev):
-        near[f, OWN] = normalize(acts[f])
+    near[0, OWN] = normalize(acts[0])
 
     pl.semaphore_wait(
         barrier, frame_size + 1 + gives_relay.astype(jnp.int32) + has_relayed.astype(jnp.int32)
@@ -137,6 +135,8 @@
         return halo(f, half, DIRECT + side + odd - 2 * side * odd, mate, FAR)
 
     for f in range(frames_dev):
+        if f > 0:
+            near[f, OWN] = normalize(acts[f])
         for half in range(halves):
             to_across(f, half).start()
             to_mate(f, half).start()
@@ -152,11 +152,12 @@
 
     size = frames * share
     lane = lax.broadcasted_iota(jnp.int32, (frames, PAIR), 1)
-    row = lax.broadcasted_iota(jnp.int32, (frames, PAIR), 0)
     frequency = jnp.exp((lane & (HEAD // 2 - 1)).astype(F32) * (-math.log(10000.0) / (HEAD // 2)))
     position = jnp.zeros((frames, PAIR), F32)
+    row = lax.broadcasted_iota(jnp.int32, (frames, PAIR), 0)
     for g in range(frames):
-        position = jnp.where(row == g, frame_index[g].astype(F32), position)
+        at = (g % frames_dev) * frame_size + g // frames_dev
+        position = jnp.where(row == at, frame_index[g].astype(F32), position)
     angle = position * frequency
     for table, entries in ((cosine, jnp.cos(angle)), (sine, jnp.sin(angle))):
         table[...] = jnp.broadcast_to(entries[:, None, :], (frames, share, PAIR)).reshape(
@@ -228,7 +229,7 @@
         first = part * (block // parts) + peer * share
         return pltpu.make_async_remote_copy(
             src_ref=hidden.at[f, pl.ds(pl.multiple_of(first, 16), share)],
-            dst_ref=gathered.at[part, slot * frames_dev + f],
+            dst_ref=gathered.at[f, part, slot],
             send_sem=frame_send.at[f, part, peer],
             recv_sem=frame_recv.at[f, part, slot],
             device_id=(me, peer),
@@ -239,7 +240,7 @@
         peer = exclusive(slot, step, frame_size)
         return pltpu.make_async_remote_copy(
             src_ref=hidden.at[f, pl.ds(0, share)],
-            dst_ref=gathered.at[part, peer * frames_dev + f],
+            dst_ref=gathered.at[f, part, peer],
             send_sem=frame_send.at[f, part, peer],
             recv_sem=frame_recv.at[f, part, peer],
             device_id=(me, peer),
@@ -281,15 +282,20 @@
             for step in range(frame_size - 1, 0, -1):
                 frame_copy(f, part, step).start()
             mine = pl.ds(pl.multiple_of(part * (block // parts) + slot * share, 16), share)
-            gathered[part, slot * frames_dev + f] = hidden[f, mine]
+            gathered[f, part, slot] = hidden[f, mine]
 
     weights[0].wait()
+    for copy in weights[1:]:
+        copy.start()
     for f in range(frames_dev):
         query[f] = jnp.dot(near[f, OWN], sqkv[:, :width], preferred_element_type=F32).astype(BF16)
+    for f in range(frames_dev):
         for half in range(halves):
             to_mate(f, half).wait_recv()
-        project(f, OWN, 2)
-        pass_on(0, f)
+    pass_on(0, 0)
+    project(0, OWN, 2)
+    pass_on(0, 1)
+    project(1, OWN, 2)
     project(0, DIRECT, 1)
     begin(0)
     pass_on(1, 0)
@@ -327,44 +333,70 @@
             device_id_type=pl.DeviceIdType.MESH,
         )
 
-    weights[2].wait()
-    weights[3].wait()
-    for part in range(parts):
-        for f in range(frames_dev):
-            for step in range(1, frame_size):
-                frame_arrival(f, part, step).wait_recv()
-        renormed = normalize(gathered[part].reshape(size, width))
+    level = frame_size * share
+
+    def arrive(f, part):
+        for step in range(1, frame_size):
+            frame_arrival(f, part, step).wait_recv()
+
+    def time_project(f, first, many):
+        renormed = normalize(gathered[f, first : first + many].reshape(many * level, width))
+        span_rows = slice(f * level, (f + 1) * level)
+        turning = jnp.concatenate([cosine[span_rows]] * many, axis=0)
+        crossing = jnp.concatenate([sine[span_rows]] * many, axis=0)
         for third, target in ((0, tquery), (1, tkeys), (2, tvalues)):
             projected = jnp.dot(
                 renormed, tqkv[:, third * width : (third + 1) * width], preferred_element_type=F32
             ).astype(BF16)
-            if third == 2:
-                target[...] = projected
-            else:
-                for pair in range(heads):
-                    span = slice(pair * PAIR, (pair + 1) * PAIR)
-                    piece = projected[:, span]
+            for pair in range(heads):
+                span = slice(pair * PAIR, (pair + 1) * PAIR)
+                piece = projected[:, span]
+                if third < 2:
                     turned = jnp.dot(piece, turn, preferred_element_type=F32)
-                    target[:, span] = (
-                        piece.astype(F32) * cosine[...] + turned * sine[...]
-                    ).astype(BF16)
+                    piece = (piece.astype(F32) * turning + turned * crossing).astype(BF16)
+                for part in range(many):
+                    target[first + part, span_rows, span] = piece[part * level : (part + 1) * level]
+
+    weights[2].wait()
+    for f in range(frames_dev - 1):
+        for part in range(parts):
+            arrive(f, part)
+        time_project(f, 0, parts)
+    weights[3].wait()
+    for part in range(parts):
+        arrive(frames_dev - 1, part)
+        time_project(frames_dev - 1, part, 1)
         for apart in range(frame_size // 2 - 1, -1, -1):
             first = 2 * exclusive(slot // 2, apart, frame_size // 2)
-            rows = pl.ds(pl.multiple_of(first * chunk, 16), 2 * chunk)
+            rows = [
+                pl.ds(pl.multiple_of(f * level + first * share, 16), 2 * share)
+                for f in range(frames_dev)
+            ]
             pieces = []
             for pair in range(heads):
                 span = slice(pair * PAIR, (pair + 1) * PAIR)
                 _, time_total, time_count = attend(
-                    tquery[rows, span], tkeys[:, span], tvalues[:, span], same[...]
+                    jnp.concatenate([tquery[part, at, span] for at in rows], axis=0),
+                    tkeys[part, :, span],
+                    tvalues[part, :, span],
+                    same[...],
                 )
                 pieces.append((time_total / time_count).astype(BF16))
             time_mix = jnp.concatenate(pieces, axis=1)
-            before = gathered[part, pl.ds(first * frames_dev, 2 * frames_dev)]
+            before = jnp.concatenate(
+                [
+                    gathered[f, part, pl.ds(first, 2)].reshape(2 * share, width)
+                    for f in range(frames_dev)
+                ],
+                axis=0,
+            )
             after = (
-                before.reshape(2 * chunk, width).astype(F32)
-                + jnp.dot(time_mix, tout[...], preferred_element_type=F32)
+                before.astype(F32) + jnp.dot(time_mix, tout[...], preferred_element_type=F32)
             ).astype(BF16)
-            staged[part, pl.ds(first, 2)] = after.reshape(2, frames_dev, share, width)
+            for f in range(frames_dev):
+                for d in range(2):
+                    at = (2 * f + d) * share
+                    staged[part, first + d, f] = after[at : at + share]
             if apart > 0:
                 back_copy(part, first).start()
                 back_copy(part, first + 1).start()
@@ -429,12 +461,12 @@
                 pltpu.VMEM((frames_dev, 5 * block, width), BF16),
                 pltpu.VMEM((block, width), BF16),
                 pltpu.VMEM((frames_dev, block, width), BF16),
-                pltpu.VMEM((parts, frames, share, width), BF16),
+                pltpu.VMEM((frames_dev, parts, frame_size, share, width), BF16),
                 pltpu.VMEM((parts, frame_size, frames_dev, share, width), BF16),
                 pltpu.VMEM((frames_dev, block, width), BF16),
-                pltpu.VMEM((size, width), BF16),
-                pltpu.VMEM((size, width), BF16),
-                pltpu.VMEM((size, width), BF16),
+                pltpu.VMEM((parts, size, width), BF16),
+                pltpu.VMEM((parts, size, width), BF16),
+                pltpu.VMEM((parts, size, width), BF16),
                 pltpu.VMEM((size, PAIR), F32),
                 pltpu.VMEM((size, PAIR), F32),
                 pltpu.VMEM((4 * frames_dev * share, size), F32),

time: 41.1 us -> 41.7 us (1.015)
  no operation moved by 1% of the time
where the time goes in v5:
time: 41.7 us; the launch traced here: 41.1 us
  Pallas kernels  39.3 us (94%)
  local copies, waits for them, and re-layouts  1.77 us (4%)
    pallas_call x1, Pallas kernels, shards(): pl.pallas_call(functools.partial(kernel, res_size, frame_size), out_shape...  39.3 us
    unnamed x1, local copies, waits for them, and re-layouts  1.77 us

profile of v5, /device:TPU:3, one launch (start us, length us, event | category | flops | bytes accessed | tf_op | source)
XLA Modules:
  0.0 41.1 jit_solution(4493270494630908406)
XLA Ops:
  0.0 39.3 %shard_map.73 = bf16[2,128,768]{2,1,0:T(8,128)(2,1)} custom-call(bf16[2,128,768]{2,1,0:T(8,128)(2,1)} %acts_in.1, s32[8,5]{1,0:T(8,128)} %contacts.1, s32[8]{0:T(128)} %frame_index.1, bf16[768,2304]{1,0:T(8,128)(2,1)} %sqkv_in.1, bf16[768,768]{1,0:T(8,128)(2,1)} %sout_in.1, bf16[768,2304]{1,0:T(8,128)(2,1)} %tqkv_in.1, bf16[768,768]{1,0:T(8,128)(2,1)} %tout_in.1), custom_call_target="tpu_custom_call" | custom-call | tf_op jit(solution)/shard_map/pallas_call | solution.py:447
  39.3 1.8 %copy.9 = bf16[2,128,768]{2,1,0:T(8,128)(2,1)} copy(bf16[2,128,768]{2,1,0:T(8,128)(2,1)} %shard_map.73) | data formatting | bytes 786432

commit v6 on v5

--- a/solution.py
+++ b/solution.py
@@ -297,10 +297,10 @@
     pass_on(0, 1)
     project(1, OWN, 2)
     project(0, DIRECT, 1)
+    pass_on(1, 0)
     begin(0)
-    pass_on(1, 0)
+    pass_on(1, 1)
     take_relayed(0)
-    pass_on(1, 1)
     take_far(0)
     weights[1].wait()
     spatial(0, 0, parts)

time: 41.7 us -> 41.1 us (0.986)
  Pallas kernels: 39.3 us -> 38.7 us
    pallas_call x1, Pallas kernels: 39.3 us -> 38.7 us  [shards(): pl.pallas_call(functools.partial(kernel, res_size, frame_size), out_shape...]
where the time goes in v6:
time: 41.1 us; the launch traced here: 40.4 us
  Pallas kernels  38.7 us (94%)
  local copies, waits for them, and re-layouts  1.77 us (4%)
    pallas_call x1, Pallas kernels, shards(): pl.pallas_call(functools.partial(kernel, res_size, frame_size), out_shape...  38.7 us
    unnamed x1, local copies, waits for them, and re-layouts  1.77 us

profile of v6, /device:TPU:3, one launch (start us, length us, event | category | flops | bytes accessed | tf_op | source)
XLA Modules:
  0.0 40.4 jit_solution(17019331018868454720)
XLA Ops:
  0.0 38.7 %shard_map.73 = bf16[2,128,768]{2,1,0:T(8,128)(2,1)} custom-call(bf16[2,128,768]{2,1,0:T(8,128)(2,1)} %acts_in.1, s32[8,5]{1,0:T(8,128)} %contacts.1, s32[8]{0:T(128)} %frame_index.1, bf16[768,2304]{1,0:T(8,128)(2,1)} %sqkv_in.1, bf16[768,768]{1,0:T(8,128)(2,1)} %sout_in.1, bf16[768,2304]{1,0:T(8,128)(2,1)} %tqkv_in.1, bf16[768,768]{1,0:T(8,128)(2,1)} %tout_in.1), custom_call_target="tpu_custom_call" | custom-call | tf_op jit(solution)/shard_map/pallas_call | solution.py:447
  38.7 1.8 %copy.9 = bf16[2,128,768]{2,1,0:T(8,128)(2,1)} copy(bf16[2,128,768]{2,1,0:T(8,128)(2,1)} %shard_map.73) | data formatting | bytes 786432

commit v7 on v6

--- a/solution.py
+++ b/solution.py
@@ -300,11 +300,11 @@
     pass_on(1, 0)
     begin(0)
     pass_on(1, 1)
+    project(1, DIRECT, 1)
     take_relayed(0)
     take_far(0)
     weights[1].wait()
     spatial(0, 0, parts)
-    project(1, DIRECT, 1)
     begin(1)
     take_relayed(1)
     take_far(1)

time: 41.1 us -> 40.8 us (level)
  no operation moved by 1% of the time
where the time goes in v7:
time: 40.8 us; the launch traced here: 40 us
  Pallas kernels  38.3 us (94%)
  local copies, waits for them, and re-layouts  1.77 us (4%)
    pallas_call x1, Pallas kernels, shards(): pl.pallas_call(functools.partial(kernel, res_size, frame_size), out_shape...  38.3 us
    unnamed x1, local copies, waits for them, and re-layouts  1.77 us

profile of v7, /device:TPU:3, one launch (start us, length us, event | category | flops | bytes accessed | tf_op | source)
XLA Modules:
  0.0 40.0 jit_solution(14690385387899192121)
XLA Ops:
  0.0 38.3 %shard_map.73 = bf16[2,128,768]{2,1,0:T(8,128)(2,1)} custom-call(bf16[2,128,768]{2,1,0:T(8,128)(2,1)} %acts_in.1, s32[8,5]{1,0:T(8,128)} %contacts.1, s32[8]{0:T(128)} %frame_index.1, bf16[768,2304]{1,0:T(8,128)(2,1)} %sqkv_in.1, bf16[768,768]{1,0:T(8,128)(2,1)} %sout_in.1, bf16[768,2304]{1,0:T(8,128)(2,1)} %tqkv_in.1, bf16[768,768]{1,0:T(8,128)(2,1)} %tout_in.1), custom_call_target="tpu_custom_call" | custom-call | tf_op jit(solution)/shard_map/pallas_call | solution.py:447
  38.3 1.8 %copy.9 = bf16[2,128,768]{2,1,0:T(8,128)(2,1)} copy(bf16[2,128,768]{2,1,0:T(8,128)(2,1)} %shard_map.73) | data formatting | bytes 786432
